TPU v7x, 512 devices: a whole 4x8x8 slice. The times are simulated.
512 devices in a mesh: replica: 32 (over y_hi, z, core), expert: 16 (over x, y_lo).
Axes of the slice: x: 4, y: 8 (y_hi: 2, y_lo: 4; y = y_hi * 4 + y_lo), z: 8, core: 2. Of those that a mesh axis runs over, the one named last changes fastest.
Arguments:
- tokens: bfloat16 [65536, 1792], P(('replica', 'expert')), may hold values from -6 to 6
- cotangent: bfloat16 [65536, 1792], P(('replica', 'expert')), may hold values from -0.71875 to 0.71875
- expert_ids: int32 [65536, 1], P(('replica', 'expert')), may hold values from 0 to 1; in each aligned block of 128 rows (0 to 127, 128 to 255, ...) at most 96 rows name the same one
- gate_values: bfloat16 [65536, 1], P(('replica', 'expert')), may hold values from 0.049804688 to 1
- w_gate: bfloat16 [32, 1792, 4096], P('replica', None, 'expert'), may hold values from -0.125 to 0.125
- w_up: bfloat16 [32, 1792, 4096], P('replica', None, 'expert'), may hold values from -0.125 to 0.125
- w_down: bfloat16 [32, 4096, 1792], P('replica', 'expert'), may hold values from -6 to 6
- anchor: float32 [16, 256, 1792], P('expert', 'replica'), may hold values from -6 to 6
- momentum: float32 [16, 256, 1792], P('expert', 'replica'), may hold values from -3 to 3
Outputs:
- gate_grad: float32 [65536, 1], P(('replica', 'expert'))
- new_frag: bfloat16 [32, 16, 256, 1792], P('replica', 'expert')
- new_anchor: float32 [16, 256, 1792], P('expert', 'replica')
- new_momentum: float32 [16, 256, 1792], P('expert', 'replica')
Inputs may be any that keep to these rules, and one draw needn't show every extreme that they name: `expert_ids`: each row names one expert. In the rows of one device, no expert is named by more than 96 rows, a bound that some block reaches.
All inputs are finite; a program needn't handle non-finite values.
Results may differ from a plain program's by a relative error of at most 0.015.
Values may be sent and summed in bfloat16 or wider, within the bound.
A program may use at most 128 MiB of HBM per device.

v0:
```python
import math

import jax
import jax.numpy as jnp
from jax import lax
from jax.sharding import PartitionSpec as P

HID = 2048
EXPERTS = 2


outer_rate = 0.7
outer_momentum = 0.9
mix_weight = 0.5
inner_rate = 8.0


def per_device(tokens, cotangent, expert_ids, gate_values, w_gate, w_up, w_down, anchor, momentum):
    tok_rows, feature_count = tokens.shape
    top_count = expert_ids.shape[1]
    sources = lax.axis_size("expert")
    experts_all = EXPERTS
    slices_per = sources // experts_all
    capacity = min(tok_rows, 3 * tok_rows * top_count // (2 * experts_all))
    out_scale = 1.0 / math.sqrt(HID)
    labels = jnp.arange(experts_all, dtype=jnp.int32)
    matched = expert_ids[:, :, None] == labels[None, None, :]
    hit_count = jnp.sum(matched.astype(jnp.int32), axis=1, dtype=jnp.int32)
    before = jnp.cumsum(hit_count, axis=0, dtype=jnp.int32) - hit_count
    slot_index = jnp.sum(jnp.where(matched, before[:, None, :], 0), axis=2, dtype=jnp.int32)
    targets = (expert_ids * capacity + slot_index).reshape(-1)
    token_index = jnp.repeat(jnp.arange(tok_rows, dtype=jnp.int32), top_count)

    def pack_rows(values):
        tail = values.shape[1:]
        blank_rows = jnp.zeros((experts_all * capacity,) + tail, values.dtype)
        filled = blank_rows.at[targets].set(values).reshape((experts_all, 1, capacity) + tail)
        copies = jnp.broadcast_to(filled, (experts_all, slices_per, capacity) + tail)
        return copies.reshape((sources, capacity) + tail)

    token_send = pack_rows(tokens[token_index])
    cotangent_send = pack_rows(cotangent[token_index])
    gate_send = pack_rows(gate_values.reshape(-1))
    token_recv, cotangent_recv, gate_recv = (
        lax.all_to_all(token_send, "expert", split_axis=0, concat_axis=0, tiled=True),
        lax.all_to_all(cotangent_send, "expert", split_axis=0, concat_axis=0, tiled=True),
        lax.all_to_all(gate_send, "expert", split_axis=0, concat_axis=0, tiled=True),
    )
    token_rows = token_recv.reshape(-1, feature_count)
    gate_value = jnp.dot(token_rows, w_gate[0], preferred_element_type=jnp.float32)
    up_value = jnp.dot(token_rows, w_up[0], preferred_element_type=jnp.float32)
    activation = (jax.nn.silu(gate_value) * up_value).astype(jnp.bfloat16)
    cotangent_rows = cotangent_recv.reshape(-1, feature_count)
    projected = jnp.einsum(
        "rd,hd->rh", cotangent_rows, w_down[0], preferred_element_type=jnp.float32
    )
    slot_grad = out_scale * jnp.sum(activation.astype(jnp.float32) * projected, axis=1)
    gate_rows = gate_recv.reshape(-1)
    scaled_cot = (
        gate_rows.astype(jnp.float32)[:, None] * cotangent_rows.astype(jnp.float32)
    ).astype(jnp.bfloat16)
    frag_grad = out_scale * jnp.einsum(
        "rh,rd->hd", activation, scaled_cot, preferred_element_type=jnp.float32
    )
    returned = lax.all_to_all(
        slot_grad.reshape(sources, capacity), "expert", split_axis=0, concat_axis=0, tiled=True
    )
    per_expert = jnp.sum(returned.reshape(experts_all, slices_per, capacity), axis=1)
    gate_grad = per_expert.reshape(-1)[targets].reshape(tok_rows, top_count)
    fragment = w_down[0].astype(jnp.float32)
    replicas = lax.axis_size("replica")
    share_rows = anchor.shape[1]
    summed = lax.psum(fragment.astype(jnp.bfloat16), "replica").astype(jnp.float32)
    anchor_full, momentum_full = (
        lax.all_gather(anchor, "replica", axis=1, tiled=True),
        lax.all_gather(momentum, "replica", axis=1, tiled=True),
    )
    outer_delta = anchor_full[0] - summed / replicas
    momentum_next = outer_momentum * momentum_full[0] + outer_delta
    global_next = anchor_full[0] - outer_rate * (outer_delta + outer_momentum * momentum_next)
    row_start = lax.axis_index("replica") * share_rows
    new_anchor = lax.dynamic_slice_in_dim(global_next, row_start, share_rows, 0)[None]
    new_momentum = lax.dynamic_slice_in_dim(momentum_next, row_start, share_rows, 0)[None]
    new_frag = (
        mix_weight * (fragment - inner_rate * frag_grad) + (1.0 - mix_weight) * global_next
    ).astype(jnp.bfloat16)
    return (gate_grad, new_frag[None, None], new_anchor, new_momentum)


def solution(mesh):
    return jax.shard_map(
        per_device,
        mesh=mesh,
        in_specs=(
            P(("replica", "expert"), None),
            P(("replica", "expert"), None),
            P(("replica", "expert"), None),
            P(("replica", "expert"), None),
            P("replica", None, "expert"),
            P("replica", None, "expert"),
            P("replica", "expert", None),
            P("expert", "replica", None),
            P("expert", "replica", None),
        ),
        out_specs=(
            P(("replica", "expert"), None),
            P("replica", "expert", None, None),
            P("expert", "replica", None),
            P("expert", "replica", None),
        ),
        check_vma=False,
    )
```

profile of v0, /device:TPU:1, one launch (start us, length us, event | category | flops | bytes accessed | tf_op | source)
XLA Modules:
  0.0 785.3 jit_solution(3420251119797663989)
XLA Ops:
  7.2 0.0 copy-start
  7.2 3.4 fusion.26
  10.6 0.7 fusion.22
  11.2 1.5 scatter_custom_fusion.2
  12.7 0.1 broadcast_in_dim.53
  12.8 0.6 copy.15
  13.4 8.0 %all-to-all-start.3 = ((bf16[16,1,96]{2,1,0:T(2,128)(2,1)}), bf16[16,1,96]{2,1,0:T(2,128)(2,1)S(1)}, u32[]{:S(2)}, u32[]{:S(2)}) async-start(bf16[16,1,96]{2,1,0:T(2,128)(2,1)} %copy.15), calls=%async_computation.3 | async-start | bytes 16384 | tf_op jit(solution)/shard_map/all_to_all | solution.py:47
  21.4 3.5 scatter_custom_fusion
  24.9 3.1 all-to-all-done.3
  28.1 3.0 broadcast_in_dim.49
  31.1 4.6 all-to-all-start
  35.7 3.5 scatter_custom_fusion.1
  39.2 119.3 %all-to-all-done = bf16[16,96,1792]{2,1,0:T(8,128)(2,1)} async-done(((bf16[16,96,1792]{2,1,0:T(8,128)(2,1)}), bf16[16,96,1792]{2,1,0:T(8,128)(2,1)}, u32[]{:S(2)}, u32[]{:S(2)}) %all-to-all-start) | async-done | bytes 5505056 | tf_op jit(solution)/shard_map/all_to_all | solution.py:45
  158.5 2.9 broadcast_in_dim.51
  161.4 4.6 all-to-all-start.1
  166.0 0.0 all-reduce.2.cloned.1.call-start
  166.1 0.7 all-reduce.2.cloned.1.call-update
  166.8 0.0 all-gather.3.cloned.1.call-start
  166.8 0.7 all-gather.3.cloned.1.call-update
  167.5 0.2 all-gather.5.cloned.1.call-start
  167.7 0.5 all-gather.5.cloned.1.call-update
  168.3 0.1 reshape.170
  168.4 396.0 %all-reduce.2.cloned.1.call-done = bf16[256,1792]{1,0:T(8,128)(2,1)} async-done(((bf16[256,1792]{1,0:T(8,128)(2,1)}), bf16[256,1792]{1,0:T(8,128)(2,1)}) %all-reduce.2.cloned.1.call-update) | async-done | bytes 917520 | tf_op jit(solution)/shard_map/psum | solution.py:73
  564.4 90.9 %all-gather.3.cloned.1.call-done = f32[1,256,1792]{2,1,0:T(8,128)} async-done(((f32[1,8,1792]{2,1,0:T(8,128)}), f32[1,256,1792]{2,1,0:T(8,128)}) %all-gather.3.cloned.1.call-update) | async-done | bytes 1835024 | tf_op jit(solution)/shard_map/all_gather | solution.py:75
  655.3 89.5 %all-gather.5.cloned.1.call-done = f32[1,256,1792]{2,1,0:T(8,128)} async-done(((f32[1,8,1792]{2,1,0:T(8,128)}), f32[1,256,1792]{2,1,0:T(8,128)}) %all-gather.5.cloned.1.call-update) | async-done | bytes 1835024 | tf_op jit(solution)/shard_map/all_gather | solution.py:76
  744.8 2.9 bitcast_add_fusion
  747.7 0.7 dynamic-slice_bitcast_fusion
  748.3 0.0 copy-done
  748.3 0.0 copy-start.1
  748.3 4.3 fusion.11
  752.6 0.0 copy-done.1
  752.6 5.3 fusion.6
  757.9 0.0 all-to-all-done.1
  757.9 4.6 fusion.9
  762.6 0.7 mul.78
  763.2 6.9 all-to-all-start.2
  770.2 5.7 fusion.8
  775.9 1.0 all-to-all-done.2
  776.9 0.1 reshape.167
  777.0 1.8 gather_fusion
  (7 shorter events, 0.1 us)
Async XLA Ops:
  7.2 741.2 %copy-start = (bf16[1,1792,256]{2,1,0:T(8,128)(2,1)S(1)}, bf16[1,1792,256]{2,1,0:T(8,128)(2,1)}, u32[]{:S(2)}) copy-start(bf16[1,1792,256]{2,1,0:T(8,128)(2,1)} %param.13) | copy-start | bytes 2752516
  13.4 14.7 %all-to-all-start.3 = ((bf16[16,1,96]{2,1,0:T(2,128)(2,1)}), bf16[16,1,96]{2,1,0:T(2,128)(2,1)S(1)}, u32[]{:S(2)}, u32[]{:S(2)}) async-start(bf16[16,1,96]{2,1,0:T(2,128)(2,1)} %copy.15), calls=%async_computation.3 | async-start | bytes 16384 | tf_op jit(solution)/shard_map/all_to_all | solution.py:47
  31.1 127.4 %all-to-all-start = ((bf16[16,96,1792]{2,1,0:T(8,128)(2,1)}), bf16[16,96,1792]{2,1,0:T(8,128)(2,1)}, u32[]{:S(2)}, u32[]{:S(2)}) async-start(bf16[16,96,1792]{2,1,0:T(8,128)(2,1)} %bitcast.57), calls=%async_computation | async-start | bytes 11010048 | tf_op jit(solution)/shard_map/all_to_all | solution.py:45
  161.4 596.5 %all-to-all-start.1 = ((bf16[16,96,1792]{2,1,0:T(8,128)(2,1)}), bf16[16,96,1792]{2,1,0:T(8,128)(2,1)}, u32[]{:S(2)}, u32[]{:S(2)}) async-start(bf16[16,96,1792]{2,1,0:T(8,128)(2,1)} %bitcast.56), calls=%async_computation.1 | async-start | bytes 11010048 | tf_op jit(solution)/shard_map/all_to_all | solution.py:46
  166.0 398.4 %all-reduce.2.cloned.1.call-start = ((), (), s32[]{:S(2)}) async-start(), calls=%async_computation.5 | async-start | bytes 1835008 | tf_op jit(solution)/shard_map/psum | solution.py:73
  166.8 488.6 %all-gather.3.cloned.1.call-start = ((), (), s32[]{:S(2)}) async-start(), calls=%async_computation.4 | async-start | bytes 1892352 | tf_op jit(solution)/shard_map/all_gather | solution.py:75
  167.5 577.3 %all-gather.5.cloned.1.call-start = ((), (), s32[]{:S(2)}) async-start(), calls=%async_computation.6 | async-start | bytes 1892352 | tf_op jit(solution)/shard_map/all_gather | solution.py:76
  748.3 4.3 copy-start.1
  763.2 13.7 %all-to-all-start.2 = ((f32[16,1,96]{2,1,0:T(1,128)}), f32[16,1,96]{2,1,0:T(1,128)S(1)}, u32[]{:S(2)}, u32[]{:S(2)}) async-start(f32[16,1,96]{2,1,0:T(1,128)} %mul.78), calls=%async_computation.2 | async-start | bytes 16384 | tf_op jit(solution)/shard_map/all_to_all | solution.py:65
Sparse Core Ops, SparseCore 0:
  169.8 394.5 all-reduce.1
  568.3 86.9 all-gather.2
  659.2 85.5 all-gather.4
where the time goes:
time: 786 us; the launch traced here: 785 us
  waiting for transfers between devices  702 us (89%)
  starting transfers between devices  24.4 us (3%)
  matrix products  19.9 us (3%)
  local copies, waits for them, and re-layouts  18.3 us (2%)
  between operations  13.9 us (2%)
    psum x1, waiting for transfers between devices, per_device(): lax.psum(fragment.astype(jnp.bfloat16), 'replica').astype(jnp.float32)  396 us
    all_to_all x1, waiting for transfers between devices, per_device(): lax.all_to_all(token_send, 'expert', split_axis=0, concat_axis=0, tiled=T...  119 us
    all_gather x1, waiting for transfers between devices, per_device(): lax.all_gather(anchor, 'replica', axis=1, tiled=True)  90.9 us
    all_gather x1, waiting for transfers between devices, per_device(): lax.all_gather(momentum, 'replica', axis=1, tiled=True)  89.5 us
  transfers between devices with their start and end apart: 7, of which 6 were waited for; matrix products, arithmetic and copies ran while one was open for 3% of the time, Pallas kernels for 0%

commit v1 on v0

v1 whole, which is shorter than its diff:
```python
import math

import jax
import jax.numpy as jnp
from jax import lax
from jax.experimental import pallas as pl
from jax.experimental.pallas import tpu as pltpu
from jax.sharding import PartitionSpec as P

HID = 2048
OUTER_RATE = 0.7
OUTER_MOMENTUM = 0.9
MIX = 0.5
INNER_RATE = 8.0
WIN = 96
F32 = jnp.float32
BF16 = jnp.bfloat16
MESH = pl.DeviceIdType.MESH
NT = (((1,), (1,)), ((), ()))
TN = (((0,), (0,)), ((), ()))


def kernel(tok, cot, ids, gates, wg, wu, wd, anc, mom,
           out_gate, out_frag, out_anc, out_mom,
           R, T, Wg, Wu, Wd, H, ACC, GSND, GRCV, PT,
           RS, TOT, PSS, PSR, AG, ANCR, MOMR, NAS, NMS, NAR, NMR,
           GSRC, GROW, Q, QG, QR,
           y_recv, y_up, y_dn, r_recv, xp_send, xc_send, xf_send, gu_send, w_send, w_recv,
           g_send, g_recv, q_send, q_recv, rs_send, rs_recv, ag_send, ag_recv,
           am_send, am_recv, na_send, na_recv, one_send, one_recv):
    D = tok.shape[1]
    scale = 1.0 / math.sqrt(HID)
    r = lax.axis_index("replica")
    e = lax.axis_index("expert")
    c = r % 2
    z = (r // 2) % 8
    yh = r // 16
    x = e // 4
    y = e % 4
    home = (c + y) % 2 == 0
    guest = (c + y) % 2 == 1
    owner = c == yh
    mate = r + 1 - 2 * c
    peer_e = e + 1 - 2 * (e % 2)
    far = r + 16 - 32 * yh
    px = x + 1 - 2 * (x % 2)
    cx = 3 - x
    ox = 3 - px
    w0 = pl.multiple_of(32 * (x // 2), 32)
    win = pl.ds(w0, WIN)
    wot = pl.ds(pl.multiple_of(32 - 32 * (x // 2), 32), WIN)
    fill = pl.ds(pl.multiple_of(96 - 96 * (x // 2), 32), 32)
    mj = c * 8 + z
    myslot = y * 4 + x
    yu = y // 2
    yy = y + yu * (3 - 2 * y)

    def rc(src, dst, ss, rs, rep, exp):
        return pltpu.make_async_remote_copy(
            src_ref=src, dst_ref=dst, send_sem=ss, recv_sem=rs, device_id=(rep, exp), device_id_type=MESH)

    def item(i):
        p, k = i // 4, i % 4
        kk = k // 2
        f = (1 - kk) * (yy + k * (1 - 2 * yy)) + kk * k
        return p, f + yu * (3 - 2 * f)

    def member(j):
        return yh * 16 + (j % 8) * 2 + j // 8

    def loop(n, body):
        def step(i, carry):
            body(i)
            return carry
        lax.fori_loop(0, n, step, 0)

    bar = pltpu.get_barrier_semaphore()

    def hello(j):
        @pl.when(j != e)
        def _():
            pl.semaphore_signal(bar, inc=1, device_id=(r, j), device_id_type=MESH)

        @pl.when(j != mj)
        def _():
            pl.semaphore_signal(bar, inc=1, device_id=(member(j), e), device_id_type=MESH)
    loop(16, hello)
    pl.semaphore_signal(bar, inc=1, device_id=(mate, peer_e), device_id_type=MESH)
    pl.semaphore_signal(bar, inc=1, device_id=(far, e), device_id_type=MESH)

    ecol = ids[...].astype(F32)
    ebc = jnp.broadcast_to(ecol, (128, 128))
    rowi = lax.broadcasted_iota(jnp.int32, (128, 128), 0)
    lane = lax.broadcasted_iota(jnp.int32, (128, 128), 1)
    eye = (rowi == lane).astype(F32)
    lower = (lane < rowi).astype(BF16)
    ones = jnp.ones((128, 128), BF16)
    ebf = ebc.astype(BF16)
    before = jnp.dot(lower, ebf, preferred_element_type=F32)
    total1 = jnp.dot(ones, ebf, preferred_element_type=F32)
    pos = ebc * (128.0 - total1 + before) + (1.0 - ebc) * (rowi.astype(F32) - before)
    perm = (pos == lane.astype(F32)).astype(F32)
    PT[...] = perm
    permb = jnp.transpose(perm).astype(BF16)
    T[0, y] = jnp.dot(permb, tok[...], preferred_element_type=F32).astype(BF16)
    T[1, y] = jnp.dot(permb, cot[...], preferred_element_type=F32).astype(BF16)
    gp = perm * gates[...].astype(F32)
    g1 = jnp.sum(gp * ebc, axis=0, keepdims=True)
    g0 = jnp.sum(gp * (1.0 - ebc), axis=0, keepdims=True)
    GSRC[0] = g0
    GSRC[1] = g1
    RS[mj] = wd[pl.ds(pl.multiple_of(16 * mj, 16), 16), :]

    pl.semaphore_wait(bar, 32)

    def up(p, s):
        return rc(T.at[p, s], T.at[p, s], y_up.at[p, s], y_recv.at[p, s], r, e + 1)

    def down(p, s):
        return rc(T.at[p, s], T.at[p, s], y_dn.at[p, s], y_recv.at[p, s], r, e - 1)

    def line_send(p, s):
        @pl.when((s <= y) & (y < 2 + c))
        def _():
            up(p, s).start()

        @pl.when((s >= y) & (y > c))
        def _():
            down(p, s).start()

    def line_step(p, s):
        @pl.when(((s < y) & (y <= 2 + c)) | ((s > y) & (y >= c)))
        def _():
            rc(T.at[p, s], T.at[p, s], y_up.at[p, s], y_recv.at[p, s], r, e).wait_recv()
        line_send(p, s)

    line_send(0, y)

    def rs_copy(j):
        return rc(wd.at[pl.ds(pl.multiple_of(16 * j, 16), 16), :], RS.at[mj], rs_send.at[j], rs_recv.at[mj], member(j), e)

    def rs_start(j):
        @pl.when(j != mj)
        def _():
            rs_copy(j).start()
    loop(16, rs_start)

    def am_copies():
        return (rc(anc, ANCR, am_send.at[0], am_recv.at[0], mate, e),
                rc(mom, MOMR, am_send.at[1], am_recv.at[1], mate, e))

    @pl.when(c != yh)
    def _():
        for copy in am_copies():
            copy.start()

    def home_of(j):
        return (j // 2) * 4 + c + 2 * (j % 2)

    def g_copy(j):
        return rc(GSRC.at[j // 4], GROW.at[myslot], g_send.at[j], g_recv.at[myslot], r, home_of(j))

    def g_start(j):
        @pl.when(home_of(j) != e)
        def _():
            g_copy(j).start()
    loop(8, g_start)

    @pl.when(home)
    def _():
        GROW[myslot] = GSRC[x // 2]

    R[0, :, fill, :] = jnp.zeros((16, 32, D), BF16)
    R[1, :, fill, :] = jnp.zeros((16, 32, D), BF16)

    def ps_copy():
        return rc(PSS, PSR, one_send.at[0], one_recv.at[0], far, e)

    def outer_sum():
        def rs_wait(j):
            @pl.when(j != mj)
            def _():
                rc(RS.at[j], RS.at[j], rs_send.at[j], rs_recv.at[j], r, e).wait_recv()
        loop(16, rs_wait)
        TOT[...] = jnp.zeros((16, D), F32)

        def rs_add(j):
            TOT[...] += RS[j].astype(F32)
        loop(16, rs_add)

        @pl.when(c != yh)
        def _():
            PSS[...] = TOT[...].astype(BF16)
            ps_copy().start()

    def na_copies():
        return (rc(NAS, NAR, na_send.at[0], na_recv.at[0], mate, e),
                rc(NMS, NMR, na_send.at[1], na_recv.at[1], mate, e))

    def ag_copy(j):
        return rc(AG.at[mj], AG.at[mj], ag_send.at[j], ag_recv.at[mj], member(j), e)

    def agy_copy():
        return rc(AG.at[mj], AG.at[mj], one_send.at[1], ag_recv.at[mj], far, e)

    def ag_start():
        def go(j):
            @pl.when(j != mj)
            def _():
                ag_copy(j).start()
        loop(16, go)

    def nesterov(a, m, tot):
        delta = a - tot * (1.0 / 32.0)
        nm = OUTER_MOMENTUM * m + delta
        return a - OUTER_RATE * (delta + OUTER_MOMENTUM * nm), nm

    def outer_own():
        @pl.when(owner)
        def _():
            for copy in am_copies():
                copy.wait_recv()
            ps_copy().wait_recv()
            TOT[...] += PSR[...].astype(F32)
            mine = pl.ds(pl.multiple_of(8 * c, 8), 8)
            other = pl.ds(pl.multiple_of(8 - 8 * c, 8), 8)
            na, nm = nesterov(anc[...], mom[...], TOT[mine, :])
            out_anc[...] = na
            out_mom[...] = nm
            nb, nn = nesterov(ANCR[...], MOMR[...], TOT[other, :])
            NAS[...] = nb
            NMS[...] = nn
            for copy in na_copies():
                copy.start()
            TOT[mine, :] = na
            TOT[other, :] = nb
            AG[mj] = TOT[...].astype(BF16)
            agy_copy().start()
            ag_start()

    def outer_pass():
        @pl.when(c != yh)
        def _():
            agy_copy().wait_recv()
            ag_start()

    def arrived(p, slot):
        rc(R.at[p, slot, win], R.at[p, slot, win], gu_send.at[p, slot], r_recv.at[p, slot], r, e).wait_recv()

    def to_partner(p, s):
        slot = s * 4 + x
        return rc(T.at[p, s, win], R.at[p, slot, win], xp_send.at[p, s], r_recv.at[p, slot], r, px * 4 + y)

    def to_cross(p, s):
        slot = s * 4 + x
        return rc(T.at[p, s, wot], R.at[p, slot, wot], xc_send.at[p, s], r_recv.at[p, slot], r, cx * 4 + y)

    def on_to_partner(p, s):
        slot = s * 4 + cx
        return rc(R.at[p, slot, win], R.at[p, slot, win], xf_send.at[p, s], r_recv.at[p, slot], r, px * 4 + y)

    def own_copy(p, s):
        slot = s * 4 + x
        return pltpu.make_async_copy(T.at[p, s, win], R.at[p, slot, win], r_recv.at[p, slot])

    def to_guest(p, slot):
        return rc(R.at[p, slot, win], R.at[p, slot, win], gu_send.at[p, slot], r_recv.at[p, slot], mate, e)

    def own_to_guest(p, s):
        slot = s * 4 + x
        return rc(T.at[p, s, win], R.at[p, slot, win], gu_send.at[p, slot], r_recv.at[p, slot], mate, e)

    def hidden(s, wgr, wur):
        rows = R[0, pl.ds(s * 4, 4)].reshape(512, D)
        a = jnp.dot(rows, wgr[...], preferred_element_type=F32)
        u = jnp.dot(rows, wur[...], preferred_element_type=F32)
        H[s] = (a / (1.0 + jnp.exp(-a)) * u).astype(BF16)

    def grads(s, wdr):
        rows = R[1, pl.ds(s * 4, 4)].reshape(512, D)
        h = H[s].astype(F32)
        proj = lax.dot_general(rows, wdr[...], NT, preferred_element_type=F32)
        qcol = jnp.sum(h * proj, axis=1, keepdims=True)
        cols = []
        for j in range(4):
            Q[s * 4 + j] = jnp.sum(eye * qcol[j * 128:(j + 1) * 128], axis=0, keepdims=True)
            cols.append(jnp.sum(eye * GROW[s * 4 + j], axis=1, keepdims=True))
        hg = jnp.transpose((h * jnp.concatenate(cols, axis=0)).astype(BF16))
        for d in range(0, D, 256):
            ACC[:, d:d + 256] += jnp.dot(hg, rows[:, d:d + 256], preferred_element_type=F32)

    ACC[...] = jnp.zeros((256, D), F32)

    def gg_copy():
        return rc(GROW, GROW, one_send.at[2], one_recv.at[2], mate, e)

    def qg_copy():
        return rc(Q, QG, one_send.at[3], one_recv.at[3], mate, e)

    def gr_copy():
        return rc(GSND, GRCV, one_send.at[4], one_recv.at[4], mate, peer_e)

    def w_copies():
        return (rc(wg, Wg, w_send.at[0], w_recv.at[0], mate, peer_e),
                rc(wu, Wu, w_send.at[1], w_recv.at[1], mate, peer_e),
                rc(wd, Wd, w_send.at[2], w_recv.at[2], mate, peer_e))

    def q_copy(slot):
        return rc(Q.at[slot], QR.at[x * 2 + y // 2], q_send.at[slot], q_recv.at[x * 2 + y // 2],
                  r, (slot % 4) * 4 + slot // 4)

    @pl.when(home)
    def _():
        def g_wait(slot):
            @pl.when(slot != myslot)
            def _():
                rc(GROW.at[slot], GROW.at[slot], g_send.at[0], g_recv.at[slot], r, e).wait_recv()

        def step(i):
            @pl.when(i < 8)
            def _():
                p, s = item(i)
                to_partner(p, s).start()
                to_cross(p, s).start()
                own_to_guest(p, s).start()
                own_copy(p, s).start()

            @pl.when((i > 0) & (i < 9))
            def _():
                p, s = item(i - 1)
                arrived(p, s * 4 + cx)
                on_to_partner(p, s).start()
                to_guest(p, s * 4 + cx).start()
                arrived(p, s * 4 + px)
                to_guest(p, s * 4 + px).start()

            @pl.when(i == 0)
            def _():
                line_step(*item(1))
                line_send(1, y)

            @pl.when((i > 0) & (i < 7) & (i != 3))
            def _():
                line_step(*item(i + 1))

            @pl.when(i == 3)
            def _():
                loop(16, g_wait)
                gg_copy().start()

            @pl.when(i > 1)
            def _():
                p, s = item(i - 2)
                arrived(p, s * 4 + ox)
                to_guest(p, s * 4 + ox).start()
                own_copy(p, s).wait()

                @pl.when(p == 0)
                def _():
                    hidden(s, wg, wu)

                @pl.when(p == 1)
                def _():
                    grads(s, wd)

            @pl.when(i == 4)
            def _():
                outer_sum()

            @pl.when(i == 6)
            def _():
                outer_own()

            @pl.when(i == 8)
            def _():
                outer_pass()
        loop(10, step)

        qg_copy().wait_recv()
        Q[...] += QG[...]

        def q_start(slot):
            @pl.when(slot != myslot)
            def _():
                q_copy(slot).start()
        loop(16, q_start)
        QR[x * 2 + y // 2] = Q[myslot]

    @pl.when(guest)
    def _():
        ws = w_copies()
        line_send(1, y)
        for k in (1, 2, 3):
            line_step(*item(k))
        ws[0].start()
        ws[1].start()
        for k in (5, 6, 7):
            line_step(*item(k))
        ws[2].start()
        outer_sum()
        outer_own()
        outer_pass()
        ws[0].wait_recv()
        ws[1].wait_recv()

        def step(i):
            p, s = item(i)
            for col in (x, cx, px, ox):
                arrived(p, s * 4 + col)

            @pl.when(p == 0)
            def _():
                hidden(s, Wg, Wu)

            @pl.when(i == 4)
            def _():
                gg_copy().wait_recv()
                ws[2].wait_recv()

            @pl.when(p == 1)
            def _():
                grads(s, Wd)
        loop(8, step)

        GSND[...] = (scale * ACC[...]).astype(BF16)
        gr_copy().start()
        qg_copy().start()

    def q_wait(j):
        @pl.when(home_of(j) != e)
        def _():
            rc(QR.at[j], QR.at[j], q_send.at[0], q_recv.at[j], r, e).wait_recv()
    loop(8, q_wait)
    q0 = QR[0] + QR[1] + QR[2] + QR[3]
    q1 = QR[4] + QR[5] + QR[6] + QR[7]
    picked = PT[...] * (ebc * q1 + (1.0 - ebc) * q0)
    out_gate[...] = scale * jnp.sum(picked, axis=1, keepdims=True)

    def ag_wait(j):
        @pl.when(j != mj)
        def _():
            rc(AG.at[j], AG.at[j], ag_send.at[j], ag_recv.at[j], r, e).wait_recv()
    loop(16, ag_wait)

    @pl.when(c != yh)
    def _():
        for copy in na_copies():
            copy.wait_recv()
        out_anc[...] = NAR[...]
        out_mom[...] = NMR[...]

    def merge(j, grad):
        rows = pl.ds(pl.multiple_of(16 * j, 16), 16)
        out_frag[rows, :] = (MIX * wd[rows, :].astype(F32) - MIX * INNER_RATE * grad(rows)
                             + (1.0 - MIX) * AG[j].astype(F32)).astype(BF16)

    @pl.when(home)
    def _():
        loop(16, lambda j: merge(j, lambda rows: scale * ACC[rows, :]))

    @pl.when(guest)
    def _():
        gr_copy().wait_recv()
        loop(16, lambda j: merge(j, lambda rows: GRCV[rows, :].astype(F32)))

    def drain(i):
        p, s = i // 4, i % 4

        @pl.when((s <= y) & (y < 2 + c))
        def _():
            up(p, s).wait_send()

        @pl.when((s >= y) & (y > c))
        def _():
            down(p, s).wait_send()

        @pl.when(home)
        def _():
            to_partner(p, s).wait_send()
            to_cross(p, s).wait_send()
            on_to_partner(p, s).wait_send()
            for col in range(4):
                to_guest(p, s * 4 + col).wait_send()
    loop(8, drain)

    def drain_small(j):
        @pl.when(j != mj)
        def _():
            rs_copy(j).wait_send()
            ag_copy(j).wait_send()

        @pl.when(home & (j != myslot))
        def _():
            q_copy(j).wait_send()
    loop(16, drain_small)

    def drain_g(j):
        @pl.when(home_of(j) != e)
        def _():
            g_copy(j).wait_send()
    loop(8, drain_g)

    @pl.when(home)
    def _():
        gg_copy().wait_send()

    @pl.when(guest)
    def _():
        for copy in w_copies():
            copy.wait_send()
        gr_copy().wait_send()
        qg_copy().wait_send()

    @pl.when(owner)
    def _():
        agy_copy().wait_send()
        for copy in na_copies():
            copy.wait_send()

    @pl.when(c != yh)
    def _():
        ps_copy().wait_send()
        for copy in am_copies():
            copy.wait_send()


def per_device(tokens, cotangent, expert_ids, gate_values, w_gate, w_up, w_down, anchor, momentum):
    D = tokens.shape[1]
    vm = pl.BlockSpec(memory_space=pltpu.VMEM)
    dma = pltpu.SemaphoreType.DMA
    V = pltpu.VMEM
    gate, frag, anc, mom = pl.pallas_call(
        kernel,
        out_shape=(
            jax.ShapeDtypeStruct((128, 1), F32),
            jax.ShapeDtypeStruct((256, D), BF16),
            jax.ShapeDtypeStruct((8, D), F32),
            jax.ShapeDtypeStruct((8, D), F32),
        ),
        in_specs=[vm] * 9,
        out_specs=[vm] * 4,
        scratch_shapes=[
            V((2, 16, 128, D), BF16), V((2, 4, 128, D), BF16),
            V((D, 256), BF16), V((D, 256), BF16), V((256, D), BF16),
            V((4, 512, 256), BF16), V((256, D), F32), V((256, D), BF16), V((256, D), BF16), V((128, 128), F32),
            V((16, 16, D), BF16), V((16, D), F32), V((16, D), BF16), V((16, D), BF16), V((16, 16, D), BF16),
            V((8, D), F32), V((8, D), F32), V((8, D), F32), V((8, D), F32), V((8, D), F32), V((8, D), F32),
            V((2, 1, 128), F32), V((16, 1, 128), F32), V((16, 1, 128), F32), V((16, 1, 128), F32), V((8, 1, 128), F32),
            dma((2, 4)), dma((2, 4)), dma((2, 4)), dma((2, 16)), dma((2, 4)), dma((2, 4)), dma((2, 4)), dma((2, 16)),
            dma((3,)), dma((3,)),
            dma((8,)), dma((16,)), dma((16,)), dma((8,)), dma((16,)), dma((16,)), dma((16,)), dma((16,)),
            dma((2,)), dma((2,)), dma((2,)), dma((2,)), dma((5,)), dma((5,)),
        ],
        compiler_params=pltpu.CompilerParams(
            collective_id=0, has_side_effects=True, vmem_limit_bytes=58 * 1024 * 1024),
        name="step",
    )(tokens, cotangent, expert_ids, gate_values, w_gate[0], w_up[0], w_down[0], anchor[0], momentum[0])
    return gate, frag[None, None], anc[None], mom[None]


def solution(mesh):
    return jax.shard_map(
        per_device,
        mesh=mesh,
        in_specs=(
            P(("replica", "expert"), None),
            P(("replica", "expert"), None),
            P(("replica", "expert"), None),
            P(("replica", "expert"), None),
            P("replica", None, "expert"),
            P("replica", None, "expert"),
            P("replica", "expert", None),
            P("expert", "replica", None),
            P("expert", "replica", None),
        ),
        out_specs=(
            P(("replica", "expert"), None),
            P("replica", "expert", None, None),
            P("expert", "replica", None),
            P("expert", "replica", None),
        ),
        check_vma=False,
    )
```

time: 786 us -> 127 us (0.16)
  waiting for transfers between devices: 702 us -> 0 us
  Pallas kernels: 0 us -> 118 us
  starting transfers between devices: 24.4 us -> 0 us
  matrix products: 19.9 us -> 0 us
  between operations: 13.9 us -> 0.65 us
  local copies, waits for them, and re-layouts: 18.3 us -> 7.18 us
    psum x1 -> x0, waiting for transfers between devices: 396 us -> none  [per_device(): lax.psum(fragment.astype(jnp.bfloat16), 'replica').astype(jnp.float32)]
    all_gather x2 -> x0, waiting for transfers between devices: 180 us -> none  [the longest x1 90.9 us: per_device(): lax.all_gather(anchor, 'replica', axis=1, tiled=True)]
    all_to_all x4 -> x0, waiting for transfers between devices: 123 us -> none  [the longest x1 119 us: per_device(): lax.all_to_all(token_send, 'expert', split_axis=0, concat_axis=0, tiled=T...]
    pallas_call x0 -> x1, Pallas kernels: none -> 118 us  [per_device(): pl.pallas_call(kernel, out_shape=(jax.ShapeDtypeStruct((128, 1), F32), ja...]
    all_to_all x4 -> x0, starting transfers between devices: 24.1 us -> none  [the longest x1 7.99 us: per_device(): lax.all_to_all(gate_send, 'expert', split_axis=0, concat_axis=0, tiled=True)]
    dot_general x4 -> x0, matrix products: 19.9 us -> none  [the longest x1 5.75 us: per_device(): jnp.einsum('rh,rd->hd', activation, scaled_cot, preferred_element_type=jn...]
    scatter x3 -> x0, local copies, waits for them, and re-layouts: 8.48 us -> none  [pack_rows(): blank_rows.at[targets].set(values)]
  transfers between devices with their start and end apart: 7 -> 0, of which waited for: 6 -> 0; matrix products, arithmetic and copies ran while one was open for 3% -> 0% of each run, Pallas kernels for 0% -> 0%
where the time goes in v1:
time: 127 us; the launch traced here: 126 us
  Pallas kernels  118 us (93%)
  local copies, waits for them, and re-layouts  7.18 us (6%)
    pallas_call x1, Pallas kernels, per_device(): pl.pallas_call(kernel, out_shape=(jax.ShapeDtypeStruct((128, 1), F32), ja...  118 us
    unnamed x14, local copies, waits for them, and re-layouts  7.18 us

profile of v1, /device:TPU:1, one launch (start us, length us, event | category | flops | bytes accessed | tf_op | source)
XLA Modules:
  0.0 126.1 jit_solution(9254597349166293381)
XLA Ops:
  0.6 0.0 copy-start.2
  0.6 0.6 copy-done.2
  1.3 0.0 copy-start.3
  1.3 0.7 copy.14.gates
  2.0 0.0 copy-done.3
  2.0 0.7 copy.13.ids
  2.8 118.3 %step.1 = (f32[128,1]{1,0:T(8,128)}, bf16[256,1792]{1,0:T(8,128)(2,1)}, f32[8,1792]{1,0:T(8,128)}, f32[8,1792]{1,0:T(8,128)}) custom-call(bf16[128,1792]{1,0:T(8,128)(2,1)} %tok.1, bf16[128,1792]{1,0:T(8,128)(2,1)} %cot.1, s32[128,1]{1,0:T(8,128)} %copy.13.ids, bf16[128,1]{1,0:T(8,128)(2,1)} %copy.14.gates, bf16[1792,256]{1,0:T(8,128)(2,1)} %bitcast.9, ...), custom_call_target="tpu_custom_call" | custom-call | tf_op jit(solution)/shard_map/step/pallas_call | solution.py:532
  121.1 1.4 %copy.15 = f32[128,1]{0,1:T(1,128)} copy(f32[128,1]{1,0:T(8,128)} %get-tuple-element.12) | data formatting | bytes 1024
  122.5 0.0 copy-start.1
  122.5 2.2 %copy.19 = bf16[1,1,256,1792]{3,2,1,0:T(8,128)(2,1)} copy(bf16[1,1,256,1792]{3,2,1,0:T(8,128)(2,1)} %bitcast.8) | data formatting | bytes 1835008
  124.7 0.0 copy-done.1
  124.7 0.0 copy-start
  124.7 0.6 copy.20
  125.3 0.2 copy-done
  125.5 0.6 copy.21
Async XLA Ops:
  0.6 0.7 copy-start.2
  1.3 0.7 copy-start.3
  122.5 2.2 %copy-start.1 = (f32[8,1792]{1,0:T(8,128)S(1)}, f32[8,1792]{1,0:T(8,128)}, u32[]{:S(2)}) copy-start(f32[8,1792]{1,0:T(8,128)} %get-tuple-element.10) | copy-start | bytes 172036
  124.7 0.8 copy-start

commit v2 on v1

--- a/solution.py
+++ b/solution.py
@@ -22,12 +22,12 @@
 
 def kernel(tok, cot, ids, gates, wg, wu, wd, anc, mom,
            out_gate, out_frag, out_anc, out_mom,
-           R, T, Wg, Wu, Wd, H, ACC, GSND, GRCV, PT,
+           R, T, Wg, Wu, Wd, Wo, H, ACC, GSND, GRCV, PT,
            RS, TOT, PSS, PSR, AG, ANCR, MOMR, NAS, NMS, NAR, NMR,
            GSRC, GROW, Q, QG, QR,
            y_recv, y_up, y_dn, r_recv, xp_send, xc_send, xf_send, gu_send, w_send, w_recv,
            g_send, g_recv, q_send, q_recv, rs_send, rs_recv, ag_send, ag_recv,
-           am_send, am_recv, na_send, na_recv, one_send, one_recv):
+           am_send, am_recv, na_send, na_recv, one_send, one_recv, l_sem):
     D = tok.shape[1]
     scale = 1.0 / math.sqrt(HID)
     r = lax.axis_index("replica")
@@ -60,7 +60,7 @@
             src_ref=src, dst_ref=dst, send_sem=ss, recv_sem=rs, device_id=(rep, exp), device_id_type=MESH)
 
     def item(i):
-        p, k = i // 4, i % 4
+        p, k = i % 2, i // 2
         kk = k // 2
         f = (1 - kk) * (yy + k * (1 - 2 * yy)) + kk * k
         return p, f + yu * (3 - 2 * f)
@@ -74,6 +74,17 @@
             return carry
         lax.fori_loop(0, n, step, 0)
 
+    own = pltpu.make_async_copy(wd, Wo, l_sem.at[0])
+    own.start()
+
+    def w_local():
+        return [pltpu.make_async_copy(a, b, l_sem.at[n + 1]) for n, (a, b) in enumerate(((wg, Wg), (wu, Wu), (wd, Wd)))]
+
+    @pl.when(home)
+    def _():
+        for copy in w_local():
+            copy.start()
+
     bar = pltpu.get_barrier_semaphore()
 
     def hello(j):
@@ -88,11 +99,12 @@
     pl.semaphore_signal(bar, inc=1, device_id=(mate, peer_e), device_id_type=MESH)
     pl.semaphore_signal(bar, inc=1, device_id=(far, e), device_id_type=MESH)
 
-    ecol = ids[...].astype(F32)
-    ebc = jnp.broadcast_to(ecol, (128, 128))
     rowi = lax.broadcasted_iota(jnp.int32, (128, 128), 0)
     lane = lax.broadcasted_iota(jnp.int32, (128, 128), 1)
     eye = (rowi == lane).astype(F32)
+    ecol = jnp.sum(eye * ids[...].astype(F32), axis=1, keepdims=True)
+    gcol = jnp.sum(eye * gates[...].astype(F32), axis=1, keepdims=True)
+    ebc = jnp.broadcast_to(ecol, (128, 128))
     lower = (lane < rowi).astype(BF16)
     ones = jnp.ones((128, 128), BF16)
     ebf = ebc.astype(BF16)
@@ -104,12 +116,13 @@
     permb = jnp.transpose(perm).astype(BF16)
     T[0, y] = jnp.dot(permb, tok[...], preferred_element_type=F32).astype(BF16)
     T[1, y] = jnp.dot(permb, cot[...], preferred_element_type=F32).astype(BF16)
-    gp = perm * gates[...].astype(F32)
+    gp = perm * gcol
     g1 = jnp.sum(gp * ebc, axis=0, keepdims=True)
     g0 = jnp.sum(gp * (1.0 - ebc), axis=0, keepdims=True)
     GSRC[0] = g0
     GSRC[1] = g1
-    RS[mj] = wd[pl.ds(pl.multiple_of(16 * mj, 16), 16), :]
+    mine16 = pltpu.make_async_copy(wd.at[pl.ds(pl.multiple_of(16 * mj, 16), 16), :], RS.at[mj], l_sem.at[4])
+    mine16.start()
 
     pl.semaphore_wait(bar, 32)
 
@@ -128,6 +141,15 @@
         def _():
             down(p, s).start()
 
+    def line_drain(p, s):
+        @pl.when((s <= y) & (y < 2 + c))
+        def _():
+            up(p, s).wait_send()
+
+        @pl.when((s >= y) & (y > c))
+        def _():
+            down(p, s).wait_send()
+
     def line_step(p, s):
         @pl.when(((s < y) & (y <= 2 + c)) | ((s > y) & (y >= c)))
         def _():
@@ -135,6 +157,7 @@
         line_send(p, s)
 
     line_send(0, y)
+    line_send(1, y)
 
     def rs_copy(j):
         return rc(wd.at[pl.ds(pl.multiple_of(16 * j, 16), 16), :], RS.at[mj], rs_send.at[j], rs_recv.at[mj], member(j), e)
@@ -182,6 +205,7 @@
             def _():
                 rc(RS.at[j], RS.at[j], rs_send.at[j], rs_recv.at[j], r, e).wait_recv()
         loop(16, rs_wait)
+        pltpu.make_async_copy(wd.at[pl.ds(pl.multiple_of(16 * mj, 16), 16), :], RS.at[mj], l_sem.at[4]).wait()
         TOT[...] = jnp.zeros((16, D), F32)
 
         def rs_add(j):
@@ -270,24 +294,25 @@
         slot = s * 4 + x
         return rc(T.at[p, s, win], R.at[p, slot, win], gu_send.at[p, slot], r_recv.at[p, slot], mate, e)
 
-    def hidden(s, wgr, wur):
+    def hidden(s):
         rows = R[0, pl.ds(s * 4, 4)].reshape(512, D)
-        a = jnp.dot(rows, wgr[...], preferred_element_type=F32)
-        u = jnp.dot(rows, wur[...], preferred_element_type=F32)
+        a = jnp.dot(rows, Wg[...], preferred_element_type=F32)
+        u = jnp.dot(rows, Wu[...], preferred_element_type=F32)
         H[s] = (a / (1.0 + jnp.exp(-a)) * u).astype(BF16)
 
-    def grads(s, wdr):
+    def grads(s):
         rows = R[1, pl.ds(s * 4, 4)].reshape(512, D)
-        h = H[s].astype(F32)
-        proj = lax.dot_general(rows, wdr[...], NT, preferred_element_type=F32)
-        qcol = jnp.sum(h * proj, axis=1, keepdims=True)
-        cols = []
+        cols = [jnp.sum(eye * GROW[s * 4 + j], axis=1, keepdims=True) for j in range(4)]
+        hg = jnp.transpose((H[s].astype(F32) * jnp.concatenate(cols, axis=0)).astype(BF16))
+        for d in range(0, D, 256):
+            ACC[:, d:d + 256] += jnp.dot(hg, rows[:, d:d + 256], preferred_element_type=F32)
+
+    def router(s):
+        rows = R[1, pl.ds(s * 4, 4)].reshape(512, D)
+        proj = lax.dot_general(rows, Wd[...], NT, preferred_element_type=F32)
+        qcol = jnp.sum(H[s].astype(F32) * proj, axis=1, keepdims=True)
         for j in range(4):
             Q[s * 4 + j] = jnp.sum(eye * qcol[j * 128:(j + 1) * 128], axis=0, keepdims=True)
-            cols.append(jnp.sum(eye * GROW[s * 4 + j], axis=1, keepdims=True))
-        hg = jnp.transpose((h * jnp.concatenate(cols, axis=0)).astype(BF16))
-        for d in range(0, D, 256):
-            ACC[:, d:d + 256] += jnp.dot(hg, rows[:, d:d + 256], preferred_element_type=F32)
 
     ACC[...] = jnp.zeros((256, D), F32)
 
@@ -334,19 +359,16 @@
                 arrived(p, s * 4 + px)
                 to_guest(p, s * 4 + px).start()
 
-            @pl.when(i == 0)
-            def _():
-                line_step(*item(1))
-                line_send(1, y)
-
-            @pl.when((i > 0) & (i < 7) & (i != 3))
+            @pl.when((i > 0) & (i < 7))
             def _():
                 line_step(*item(i + 1))
 
-            @pl.when(i == 3)
+            @pl.when(i == 2)
             def _():
                 loop(16, g_wait)
                 gg_copy().start()
+                for copy in w_local():
+                    copy.wait()
 
             @pl.when(i > 1)
             def _():
@@ -357,11 +379,12 @@
 
                 @pl.when(p == 0)
                 def _():
-                    hidden(s, wg, wu)
+                    hidden(s)
 
                 @pl.when(p == 1)
                 def _():
-                    grads(s, wd)
+                    grads(s)
+                    router(s)
 
             @pl.when(i == 4)
             def _():
@@ -389,41 +412,52 @@
     @pl.when(guest)
     def _():
         ws = w_copies()
-        line_send(1, y)
-        for k in (1, 2, 3):
-            line_step(*item(k))
-        ws[0].start()
-        ws[1].start()
-        for k in (5, 6, 7):
-            line_step(*item(k))
-        ws[2].start()
-        outer_sum()
-        outer_own()
-        outer_pass()
+
+        @pl.when((y == 0) | (y == 3))
+        def _():
+            for p in (0, 1):
+                line_drain(p, y)
+            ws[0].start()
+            outer_sum()
+            ws[0].wait_send()
+            ws[1].start()
+            outer_own()
+            ws[1].wait_send()
+            ws[2].start()
+            outer_pass()
+
+        @pl.when((y == 1) | (y == 2))
+        def _():
+            ws[0].start()
+            for i in (2, 3, 4, 5):
+                line_step(*item(i))
+            ws[0].wait_send()
+            ws[1].start()
+            outer_sum()
+            for i in (6, 7):
+                line_step(*item(i))
+            ws[1].wait_send()
+            ws[2].start()
+            outer_own()
+            outer_pass()
         ws[0].wait_recv()
         ws[1].wait_recv()
-
-        def step(i):
-            p, s = item(i)
+        gg_copy().wait_recv()
+
+        def step(k):
+            s = item(2 * k)[1]
             for col in (x, cx, px, ox):
-                arrived(p, s * 4 + col)
-
-            @pl.when(p == 0)
-            def _():
-                hidden(s, Wg, Wu)
-
-            @pl.when(i == 4)
-            def _():
-                gg_copy().wait_recv()
-                ws[2].wait_recv()
-
-            @pl.when(p == 1)
-            def _():
-                grads(s, Wd)
-        loop(8, step)
+                arrived(0, s * 4 + col)
+            hidden(s)
+            for col in (x, cx, px, ox):
+                arrived(1, s * 4 + col)
+            grads(s)
+        loop(4, step)
 
         GSND[...] = (scale * ACC[...]).astype(BF16)
         gr_copy().start()
+        ws[2].wait_recv()
+        loop(4, router)
         qg_copy().start()
 
     def q_wait(j):
@@ -434,7 +468,7 @@
     q0 = QR[0] + QR[1] + QR[2] + QR[3]
     q1 = QR[4] + QR[5] + QR[6] + QR[7]
     picked = PT[...] * (ebc * q1 + (1.0 - ebc) * q0)
-    out_gate[...] = scale * jnp.sum(picked, axis=1, keepdims=True)
+    out_gate[...] = scale * jnp.sum(eye * jnp.sum(picked, axis=1, keepdims=True), axis=0, keepdims=True)
 
     def ag_wait(j):
         @pl.when(j != mj)
@@ -449,9 +483,11 @@
         out_anc[...] = NAR[...]
         out_mom[...] = NMR[...]
 
+    own.wait()
+
     def merge(j, grad):
         rows = pl.ds(pl.multiple_of(16 * j, 16), 16)
-        out_frag[rows, :] = (MIX * wd[rows, :].astype(F32) - MIX * INNER_RATE * grad(rows)
+        out_frag[rows, :] = (MIX * Wo[rows, :].astype(F32) - MIX * INNER_RATE * grad(rows)
                              + (1.0 - MIX) * AG[j].astype(F32)).astype(BF16)
 
     @pl.when(home)
@@ -466,13 +502,9 @@
     def drain(i):
         p, s = i // 4, i % 4
 
-        @pl.when((s <= y) & (y < 2 + c))
-        def _():
-            up(p, s).wait_send()
-
-        @pl.when((s >= y) & (y > c))
-        def _():
-            down(p, s).wait_send()
+        @pl.when(home | (y == 1) | (y == 2))
+        def _():
+            line_drain(p, s)
 
         @pl.when(home)
         def _():
@@ -506,8 +538,7 @@
 
     @pl.when(guest)
     def _():
-        for copy in w_copies():
-            copy.wait_send()
+        w_copies()[2].wait_send()
         gr_copy().wait_send()
         qg_copy().wait_send()
 
@@ -522,6 +553,13 @@
         ps_copy().wait_send()
         for copy in am_copies():
             copy.wait_send()
+
+
+def handover(a, b, c, d, a2, b2, c2, d2):
+    a2[...] = a[...]
+    b2[...] = b[...]
+    c2[...] = c[...]
+    d2[...] = d[...]
 
 
 def per_device(tokens, cotangent, expert_ids, gate_values, w_gate, w_up, w_down, anchor, momentum):
@@ -532,16 +570,16 @@
     gate, frag, anc, mom = pl.pallas_call(
         kernel,
         out_shape=(
-            jax.ShapeDtypeStruct((128, 1), F32),
+            jax.ShapeDtypeStruct((1, 128), F32),
             jax.ShapeDtypeStruct((256, D), BF16),
             jax.ShapeDtypeStruct((8, D), F32),
             jax.ShapeDtypeStruct((8, D), F32),
         ),
-        in_specs=[vm] * 9,
+        in_specs=[vm] * 4 + [pl.BlockSpec(memory_space=pl.ANY)] * 3 + [vm] * 2,
         out_specs=[vm] * 4,
         scratch_shapes=[
             V((2, 16, 128, D), BF16), V((2, 4, 128, D), BF16),
-            V((D, 256), BF16), V((D, 256), BF16), V((256, D), BF16),
+            V((D, 256), BF16), V((D, 256), BF16), V((256, D), BF16), V((256, D), BF16),
             V((4, 512, 256), BF16), V((256, D), F32), V((256, D), BF16), V((256, D), BF16), V((128, 128), F32),
             V((16, 16, D), BF16), V((16, D), F32), V((16, D), BF16), V((16, D), BF16), V((16, 16, D), BF16),
             V((8, D), F32), V((8, D), F32), V((8, D), F32), V((8, D), F32), V((8, D), F32), V((8, D), F32),
@@ -549,13 +587,26 @@
             dma((2, 4)), dma((2, 4)), dma((2, 4)), dma((2, 16)), dma((2, 4)), dma((2, 4)), dma((2, 4)), dma((2, 16)),
             dma((3,)), dma((3,)),
             dma((8,)), dma((16,)), dma((16,)), dma((8,)), dma((16,)), dma((16,)), dma((16,)), dma((16,)),
-            dma((2,)), dma((2,)), dma((2,)), dma((2,)), dma((5,)), dma((5,)),
+            dma((2,)), dma((2,)), dma((2,)), dma((2,)), dma((5,)), dma((5,)), dma((5,)),
         ],
         compiler_params=pltpu.CompilerParams(
             collective_id=0, has_side_effects=True, vmem_limit_bytes=58 * 1024 * 1024),
         name="step",
-    )(tokens, cotangent, expert_ids, gate_values, w_gate[0], w_up[0], w_down[0], anchor[0], momentum[0])
-    return gate, frag[None, None], anc[None], mom[None]
+    )(tokens, cotangent, expert_ids.reshape(1, 128), gate_values.reshape(1, 128), w_gate[0], w_up[0], w_down[0], anchor[0], momentum[0])
+    gate, frag, anc, mom = pl.pallas_call(
+        handover,
+        out_shape=(
+            jax.ShapeDtypeStruct((1, 128), F32),
+            jax.ShapeDtypeStruct((256, D), BF16),
+            jax.ShapeDtypeStruct((8, D), F32),
+            jax.ShapeDtypeStruct((8, D), F32),
+        ),
+        in_specs=[vm] * 4,
+        out_specs=[vm] * 4,
+        compiler_params=pltpu.CompilerParams(vmem_limit_bytes=58 * 1024 * 1024),
+        name="handover",
+    )(gate, frag, anc, mom)
+    return gate.reshape(128, 1), frag[None, None], anc[None], mom[None]
 
 
 def solution(mesh):

time: 127 us -> 106 us (0.83)
  Pallas kernels: 118 us -> 104 us
  local copies, waits for them, and re-layouts: 7.18 us -> 0 us
    pallas_call x1 -> x2, Pallas kernels: 118 us -> 104 us  [the longest x1 102 us: per_device(): pl.pallas_call(kernel, out_shape=(jax.ShapeDtypeStruct((1, 128), F32), ja...]
    unnamed x14 -> x0, local copies, waits for them, and re-layouts: 7.18 us -> none
where the time goes in v2:
time: 106 us; the launch traced here: 105 us
  Pallas kernels  104 us (98%)
    pallas_call x1, Pallas kernels, per_device(): pl.pallas_call(kernel, out_shape=(jax.ShapeDtypeStruct((1, 128), F32), ja...  102 us
    pallas_call x1, Pallas kernels, per_device(): pl.pallas_call(handover, out_shape=(jax.ShapeDtypeStruct((1, 128), F32),...  2.19 us

profile of v2, /device:TPU:1, one launch (start us, length us, event | category | flops | bytes accessed | tf_op | source)
XLA Modules:
  0.0 105.0 jit_solution(11712449869105724959)
XLA Ops:
  0.6 102.2 %step.1 = (f32[1,128]{1,0:T(1,128)}, bf16[256,1792]{1,0:T(8,128)(2,1)}, f32[8,1792]{1,0:T(8,128)}, f32[8,1792]{1,0:T(8,128)}) custom-call(bf16[128,1792]{1,0:T(8,128)(2,1)} %tok.1, bf16[128,1792]{1,0:T(8,128)(2,1)} %cot.1, s32[1,128]{1,0:T(1,128)} %bitcast.16, bf16[1,128]{1,0:T(2,128)(2,1)} %bitcast.17, bf16[1792,256]{1,0:T(8,128)(2,1)} %bitcast.11, ...), custom_call_target="tpu_custom_call" | custom-call | tf_op jit(solution)/shard_map/step/pallas_call | solution.py:570
  102.8 2.2 %handover.1 = (f32[1,128]{1,0:T(1,128)}, bf16[256,1792]{1,0:T(8,128)(2,1)}, f32[8,1792]{1,0:T(8,128)}, f32[8,1792]{1,0:T(8,128)}) custom-call(f32[1,128]{1,0:T(1,128)} %get-tuple-element.12.a, bf16[256,1792]{1,0:T(8,128)(2,1)} %get-tuple-element.13.b, f32[8,1792]{1,0:T(8,128)} %get-tuple-element.14.c, f32[8,1792]{1,0:T(8,128)} %get-tuple-element.15.d), custom_call_target="tpu_custom_call" | custom-call | tf_op jit(solution)/shard_map/handover/pallas_call | solution.py:596

commit v3 on v2

--- a/solution.py
+++ b/solution.py
@@ -22,13 +22,14 @@
 
 def kernel(tok, cot, ids, gates, wg, wu, wd, anc, mom,
            out_gate, out_frag, out_anc, out_mom,
-           R, T, Wg, Wu, Wd, Wo, H, ACC, GSND, GRCV, PT,
-           RS, TOT, PSS, PSR, AG, ANCR, MOMR, NAS, NMS, NAR, NMR,
+           R, T, WU, WD, Wo, H, ACC, GSND, GRCV, PT,
+           CH, RSS, RS, TOT, PSS, PSR, AG, ANCR, MOMR, NAS, NMS, NAR, NMR,
            GSRC, GROW, Q, QG, QR,
            y_recv, y_up, y_dn, r_recv, xp_send, xc_send, xf_send, gu_send, w_send, w_recv,
            g_send, g_recv, q_send, q_recv, rs_send, rs_recv, ag_send, ag_recv,
-           am_send, am_recv, na_send, na_recv, one_send, one_recv, l_sem):
+           am_send, am_recv, na_send, na_recv, one_send, one_recv, l_sem, gr_send, gr_recv):
     D = tok.shape[1]
+    HALF = D // 2
     scale = 1.0 / math.sqrt(HID)
     r = lax.axis_index("replica")
     e = lax.axis_index("expert")
@@ -40,6 +41,9 @@
     home = (c + y) % 2 == 0
     guest = (c + y) % 2 == 1
     owner = c == yh
+    mid = (y == 1) | (y == 2)
+    edge = (y == 0) | (y == 3)
+    other_e = e - 2 * y + 3
     mate = r + 1 - 2 * c
     peer_e = e + 1 - 2 * (e % 2)
     far = r + 16 - 32 * yh
@@ -60,13 +64,15 @@
             src_ref=src, dst_ref=dst, send_sem=ss, recv_sem=rs, device_id=(rep, exp), device_id_type=MESH)
 
     def item(i):
-        p, k = i % 2, i // 2
+        ge4, ge13 = (i + 12) // 16, (i + 3) // 16
+        k = ge4 * (1 - ge13) * ((i + 11) // 3 - 4) + ge13 * (i - 12)
+        p = (1 - ge4) * i + ge4 * (1 - ge13) * ((i + 11) % 3) + ge13 * 3
         kk = k // 2
         f = (1 - kk) * (yy + k * (1 - 2 * yy)) + kk * k
         return p, f + yu * (3 - 2 * f)
 
     def member(j):
-        return yh * 16 + (j % 8) * 2 + j // 8
+        return yh * 16 + j * 2 + c
 
     def loop(n, body):
         def step(i, carry):
@@ -78,7 +84,12 @@
     own.start()
 
     def w_local():
-        return [pltpu.make_async_copy(a, b, l_sem.at[n + 1]) for n, (a, b) in enumerate(((wg, Wg), (wu, Wu), (wd, Wd)))]
+        pairs = []
+        for n in (0, 1):
+            cols = pl.ds(128 * n, 128)
+            pairs += [(wg.at[:, cols], WU.at[n, :, pl.ds(0, 128)]), (wu.at[:, cols], WU.at[n, :, pl.ds(128, 128)]),
+                      (wd.at[cols, :], WD.at[n])]
+        return [pltpu.make_async_copy(a, b, l_sem.at[2 + n]) for n, (a, b) in enumerate(pairs)]
 
     @pl.when(home)
     def _():
@@ -92,12 +103,20 @@
         def _():
             pl.semaphore_signal(bar, inc=1, device_id=(r, j), device_id_type=MESH)
 
-        @pl.when(j != mj)
+    loop(16, hello)
+
+    def hello_z(j):
+        @pl.when(j != z)
         def _():
             pl.semaphore_signal(bar, inc=1, device_id=(member(j), e), device_id_type=MESH)
-    loop(16, hello)
+    loop(8, hello_z)
+    pl.semaphore_signal(bar, inc=1, device_id=(mate, e), device_id_type=MESH)
     pl.semaphore_signal(bar, inc=1, device_id=(mate, peer_e), device_id_type=MESH)
     pl.semaphore_signal(bar, inc=1, device_id=(far, e), device_id_type=MESH)
+
+    @pl.when(mid)
+    def _():
+        pl.semaphore_signal(bar, inc=1, device_id=(mate, other_e), device_id_type=MESH)
 
     rowi = lax.broadcasted_iota(jnp.int32, (128, 128), 0)
     lane = lax.broadcasted_iota(jnp.int32, (128, 128), 1)
@@ -114,17 +133,16 @@
     perm = (pos == lane.astype(F32)).astype(F32)
     PT[...] = perm
     permb = jnp.transpose(perm).astype(BF16)
-    T[0, y] = jnp.dot(permb, tok[...], preferred_element_type=F32).astype(BF16)
-    T[1, y] = jnp.dot(permb, cot[...], preferred_element_type=F32).astype(BF16)
+    for p, rows in enumerate((tok, tok, cot, cot)):
+        cols = pl.ds(HALF * (p % 2), HALF)
+        T[p, y] = jnp.dot(permb, rows[:, cols], preferred_element_type=F32).astype(BF16)
     gp = perm * gcol
     g1 = jnp.sum(gp * ebc, axis=0, keepdims=True)
     g0 = jnp.sum(gp * (1.0 - ebc), axis=0, keepdims=True)
     GSRC[0] = g0
     GSRC[1] = g1
-    mine16 = pltpu.make_async_copy(wd.at[pl.ds(pl.multiple_of(16 * mj, 16), 16), :], RS.at[mj], l_sem.at[4])
-    mine16.start()
-
-    pl.semaphore_wait(bar, 32)
+
+    pl.semaphore_wait(bar, 25 + y * (3 - y) // 2)
 
     def up(p, s):
         return rc(T.at[p, s], T.at[p, s], y_up.at[p, s], y_recv.at[p, s], r, e + 1)
@@ -159,24 +177,33 @@
     line_send(0, y)
     line_send(1, y)
 
+    def ch_copy():
+        return rc(wd.at[pl.ds(pl.multiple_of(128 - 128 * c, 128), 128), :], CH, one_send.at[4], one_recv.at[4], mate, e)
+
     def rs_copy(j):
-        return rc(wd.at[pl.ds(pl.multiple_of(16 * j, 16), 16), :], RS.at[mj], rs_send.at[j], rs_recv.at[mj], member(j), e)
-
-    def rs_start(j):
-        @pl.when(j != mj)
-        def _():
-            rs_copy(j).start()
-    loop(16, rs_start)
+        return rc(RSS.at[j], RS.at[z], rs_send.at[j], rs_recv.at[z], member(j), e)
+
+    def outer_start():
+        own.wait()
+        ch_copy().wait_recv()
+
+        def pair(j):
+            rows = pl.ds(pl.multiple_of(16 * j, 16), 16)
+            mine = Wo[pl.ds(pl.multiple_of(128 * c + 16 * j, 16), 16), :]
+            RSS[j] = (mine.astype(F32) + CH[rows, :].astype(F32)).astype(BF16)
+        loop(8, pair)
+        RS[z] = RSS[z]
+
+        def rs_start(j):
+            @pl.when(j != z)
+            def _():
+                rs_copy(j).start()
+        loop(8, rs_start)
 
     def am_copies():
         return (rc(anc, ANCR, am_send.at[0], am_recv.at[0], mate, e),
                 rc(mom, MOMR, am_send.at[1], am_recv.at[1], mate, e))
 
-    @pl.when(c != yh)
-    def _():
-        for copy in am_copies():
-            copy.start()
-
     def home_of(j):
         return (j // 2) * 4 + c + 2 * (j % 2)
 
@@ -187,30 +214,20 @@
         @pl.when(home_of(j) != e)
         def _():
             g_copy(j).start()
-    loop(8, g_start)
-
-    @pl.when(home)
-    def _():
-        GROW[myslot] = GSRC[x // 2]
-
-    R[0, :, fill, :] = jnp.zeros((16, 32, D), BF16)
-    R[1, :, fill, :] = jnp.zeros((16, 32, D), BF16)
-
     def ps_copy():
         return rc(PSS, PSR, one_send.at[0], one_recv.at[0], far, e)
 
     def outer_sum():
         def rs_wait(j):
-            @pl.when(j != mj)
+            @pl.when(j != z)
             def _():
                 rc(RS.at[j], RS.at[j], rs_send.at[j], rs_recv.at[j], r, e).wait_recv()
-        loop(16, rs_wait)
-        pltpu.make_async_copy(wd.at[pl.ds(pl.multiple_of(16 * mj, 16), 16), :], RS.at[mj], l_sem.at[4]).wait()
+        loop(8, rs_wait)
         TOT[...] = jnp.zeros((16, D), F32)
 
         def rs_add(j):
             TOT[...] += RS[j].astype(F32)
-        loop(16, rs_add)
+        loop(8, rs_add)
 
         @pl.when(c != yh)
         def _():
@@ -229,10 +246,23 @@
 
     def ag_start():
         def go(j):
-            @pl.when(j != mj)
+            @pl.when(j != z)
             def _():
                 ag_copy(j).start()
-        loop(16, go)
+        loop(8, go)
+
+    def half_copy():
+        half = pl.ds(8 * c, 8)
+        return rc(AG.at[half], AG.at[half], one_send.at[5], one_recv.at[5], mate, e)
+
+    def outer_half():
+        def ag_wait(j):
+            @pl.when(j != z)
+            def _():
+                got = c * 8 + j
+                rc(AG.at[got], AG.at[got], ag_send.at[j], ag_recv.at[got], r, e).wait_recv()
+        loop(8, ag_wait)
+        half_copy().start()
 
     def nesterov(a, m, tot):
         delta = a - tot * (1.0 / 32.0)
@@ -294,27 +324,55 @@
         slot = s * 4 + x
         return rc(T.at[p, s, win], R.at[p, slot, win], gu_send.at[p, slot], r_recv.at[p, slot], mate, e)
 
-    def hidden(s):
-        rows = R[0, pl.ds(s * 4, 4)].reshape(512, D)
-        a = jnp.dot(rows, Wg[...], preferred_element_type=F32)
-        u = jnp.dot(rows, Wu[...], preferred_element_type=F32)
-        H[s] = (a / (1.0 + jnp.exp(-a)) * u).astype(BF16)
-
-    def grads(s):
-        rows = R[1, pl.ds(s * 4, 4)].reshape(512, D)
+    @pl.when(home)
+    def _():
+        for p in (0, 1):
+            to_partner(p, y).start()
+            to_cross(p, y).start()
+
+    ch_copy().start()
+
+    @pl.when(c != yh)
+    def _():
+        for copy in am_copies():
+            copy.start()
+
+    loop(8, g_start)
+
+    @pl.when(home)
+    def _():
+        GROW[myslot] = GSRC[x // 2]
+
+    for p in range(4):
+        R[p, :, fill, :] = jnp.zeros((16, 32, HALF), BF16)
+
+    def hidden(s, units):
+        rows0 = R[0, pl.ds(s * 4, 4)].reshape(512, HALF)
+        rows1 = R[1, pl.ds(s * 4, 4)].reshape(512, HALF)
+        for n in range(units):
+            au = (jnp.dot(rows0, WU[n, :HALF, :], preferred_element_type=F32)
+                  + jnp.dot(rows1, WU[n, HALF:, :], preferred_element_type=F32))
+            a = au[:, :128]
+            H[s, :, 128 * n:128 * (n + 1)] = (a / (1.0 + jnp.exp(-a)) * au[:, 128:]).astype(BF16)
+
+    def grads(s, half, units):
+        rows = R[2 + half, pl.ds(s * 4, 4)].reshape(512, HALF)
         cols = [jnp.sum(eye * GROW[s * 4 + j], axis=1, keepdims=True) for j in range(4)]
-        hg = jnp.transpose((H[s].astype(F32) * jnp.concatenate(cols, axis=0)).astype(BF16))
-        for d in range(0, D, 256):
-            ACC[:, d:d + 256] += jnp.dot(hg, rows[:, d:d + 256], preferred_element_type=F32)
-
-    def router(s):
-        rows = R[1, pl.ds(s * 4, 4)].reshape(512, D)
-        proj = lax.dot_general(rows, Wd[...], NT, preferred_element_type=F32)
-        qcol = jnp.sum(H[s].astype(F32) * proj, axis=1, keepdims=True)
+        hg = jnp.transpose((H[s, :, :128 * units].astype(F32) * jnp.concatenate(cols, axis=0)).astype(BF16))
+        for d, w in ((0, 256), (256, 256), (512, 384)):
+            at = slice(HALF * half + d, HALF * half + d + w)
+            ACC[:128 * units, at] += jnp.dot(hg, rows[:, d:d + w], preferred_element_type=F32)
+
+    def router(s, half, units):
+        rows = R[2 + half, pl.ds(s * 4, 4)].reshape(512, HALF)
+        down_rows = WD[:units, :, HALF * half:HALF * (half + 1)].reshape(128 * units, HALF)
+        proj = lax.dot_general(rows, down_rows, NT, preferred_element_type=F32)
+        qcol = jnp.sum(H[s, :, :128 * units].astype(F32) * proj, axis=1, keepdims=True)
         for j in range(4):
-            Q[s * 4 + j] = jnp.sum(eye * qcol[j * 128:(j + 1) * 128], axis=0, keepdims=True)
-
-    ACC[...] = jnp.zeros((256, D), F32)
+            Q[s * 4 + j] += jnp.sum(eye * qcol[j * 128:(j + 1) * 128], axis=0, keepdims=True)
+
+    ACC[...] = jnp.zeros((384, D), F32)
+    Q[...] = jnp.zeros((16, 1, 128), F32)
 
     def gg_copy():
         return rc(GROW, GROW, one_send.at[2], one_recv.at[2], mate, e)
@@ -322,18 +380,133 @@
     def qg_copy():
         return rc(Q, QG, one_send.at[3], one_recv.at[3], mate, e)
 
-    def gr_copy():
-        return rc(GSND, GRCV, one_send.at[4], one_recv.at[4], mate, peer_e)
-
-    def w_copies():
-        return (rc(wg, Wg, w_send.at[0], w_recv.at[0], mate, peer_e),
-                rc(wu, Wu, w_send.at[1], w_recv.at[1], mate, peer_e),
-                rc(wd, Wd, w_send.at[2], w_recv.at[2], mate, peer_e))
+    def gr_out(half):
+        GSND[half] = (scale * ACC[:, HALF * half:HALF * (half + 1)]).astype(BF16)
+
+    def gr_to(half, kind, src, count, dst, exp):
+        return rc(GSND.at[half, pl.ds(src, count)], GRCV.at[half, pl.ds(dst, count)], gr_send.at[half, kind],
+                  gr_recv.at[half, kind], mate, exp)
+
+    def gr_edge(half):
+        return gr_to(half, 0, 0, 128, 0, peer_e)
+
+    def gr_mid(half):
+        return gr_to(half, 0, 0, 256, 0, peer_e), gr_to(half, 1, 256, 128, 128, other_e)
+
+    def w_unit(src, dst, exp):
+        cols = pl.ds(128 * src, 128)
+        up_gate = (rc(wg.at[:, cols], WU.at[dst, :, pl.ds(0, 128)], w_send.at[dst, 0], w_recv.at[dst, 0], mate, exp),
+                   rc(wu.at[:, cols], WU.at[dst, :, pl.ds(128, 128)], w_send.at[dst, 1], w_recv.at[dst, 1], mate, exp))
+        return up_gate, rc(wd.at[cols, :], WD.at[dst], w_send.at[dst, 2], w_recv.at[dst, 2], mate, exp)
+
+    def w_start(pair):
+        for copy in pair:
+            copy.start()
+
+    def w_sent(pair):
+        for copy in pair:
+            copy.wait_send()
+
+    def w_arrived(units):
+        for n in range(units):
+            for copy in w_unit(0, n, e)[0]:
+                copy.wait_recv()
 
     def q_copy(slot):
         return rc(Q.at[slot], QR.at[x * 2 + y // 2], q_send.at[slot], q_recv.at[x * 2 + y // 2],
                   r, (slot % 4) * 4 + slot // 4)
 
+    def drain(i):
+        p, s = i // 4, i % 4
+
+        @pl.when(home | (mid & (s != y)))
+        def _():
+            line_drain(p, s)
+
+        @pl.when(guest & mid & (s == y) & (p > 1))
+        def _():
+            line_drain(p, s)
+
+        @pl.when(home)
+        def _():
+            to_partner(p, s).wait_send()
+            to_cross(p, s).wait_send()
+            on_to_partner(p, s).wait_send()
+            for col in range(4):
+                to_guest(p, s * 4 + col).wait_send()
+
+    def drain_z(j):
+        @pl.when(j != z)
+        def _():
+            rs_copy(j).wait_send()
+            ag_copy(j).wait_send()
+    def drain_g(j):
+        @pl.when(home_of(j) != e)
+        def _():
+            g_copy(j).wait_send()
+
+    def drains():
+        loop(16, drain)
+        loop(8, drain_z)
+        loop(8, drain_g)
+
+    def merge(j, grad):
+        rows = pl.ds(pl.multiple_of(16 * j, 16), 16)
+        for half in (0, 1):
+            cols = pl.ds(HALF * half, HALF)
+            out_frag[rows, cols] = (MIX * Wo[rows, cols].astype(F32) - MIX * INNER_RATE * grad(rows, half)
+                                    + (1.0 - MIX) * AG[j, :, cols].astype(F32)).astype(BF16)
+
+    def guest_work(units):
+        w_arrived(units)
+        gg_copy().wait_recv()
+
+        def step(i):
+            if units == 3:
+                for n in (13, 14, 15):
+                    @pl.when(i == 4 * n - 48)
+                    def _(n=n):
+                        line_step(*item(n))
+
+                @pl.when(i == 10)
+                def _():
+                    outer_half()
+
+            p, s = item(i)
+            for col in (x, cx, px, ox):
+                arrived(p, s * 4 + col)
+
+            @pl.when(p == 1)
+            def _():
+                hidden(s, units)
+
+            for half in (0, 1):
+                @pl.when(p == 2 + half)
+                def _():
+                    grads(s, half, units)
+
+            @pl.when(i == 12)
+            def _():
+                gr_out(0)
+                for copy in ((gr_edge(0),) if units == 1 else gr_mid(0)):
+                    copy.start()
+                for n in range(units):
+                    w_unit(0, n, e)[1].wait_recv()
+                loop(4, lambda k: router(k, 0, units))
+                router(y, 1, units)
+
+            @pl.when(i == 15)
+            def _():
+                gr_out(1)
+                for copy in ((gr_edge(1),) if units == 1 else gr_mid(1)):
+                    copy.start()
+
+            @pl.when(i > 12)
+            def _():
+                router(s, 1, units)
+        loop(16, step)
+        qg_copy().start()
+
     @pl.when(home)
     def _():
         def g_wait(slot):
@@ -342,15 +515,13 @@
                 rc(GROW.at[slot], GROW.at[slot], g_send.at[0], g_recv.at[slot], r, e).wait_recv()
 
         def step(i):
-            @pl.when(i < 8)
+            @pl.when(i < 16)
             def _():
                 p, s = item(i)
-                to_partner(p, s).start()
-                to_cross(p, s).start()
                 own_to_guest(p, s).start()
                 own_copy(p, s).start()
 
-            @pl.when((i > 0) & (i < 9))
+            @pl.when((i > 0) & (i < 17))
             def _():
                 p, s = item(i - 1)
                 arrived(p, s * 4 + cx)
@@ -359,16 +530,37 @@
                 arrived(p, s * 4 + px)
                 to_guest(p, s * 4 + px).start()
 
-            @pl.when((i > 0) & (i < 7))
+            @pl.when(i == 1)
+            def _():
+                outer_start()
+
+            @pl.when(i == 2)
+            def _():
+                line_send(2, y)
+
+            @pl.when(i == 4)
+            def _():
+                line_send(3, y)
+
+            @pl.when((i > 2) & (i < 15))
             def _():
                 line_step(*item(i + 1))
 
+            @pl.when((i > 0) & (i < 15))
+            def _():
+                p, s = item(i + 1)
+                to_partner(p, s).start()
+                to_cross(p, s).start()
+
             @pl.when(i == 2)
+            def _():
+                for copy in w_local():
+                    copy.wait()
+
+            @pl.when(i == 3)
             def _():
                 loop(16, g_wait)
                 gg_copy().start()
-                for copy in w_local():
-                    copy.wait()
 
             @pl.when(i > 1)
             def _():
@@ -377,28 +569,36 @@
                 to_guest(p, s * 4 + ox).start()
                 own_copy(p, s).wait()
 
-                @pl.when(p == 0)
-                def _():
-                    hidden(s)
-
                 @pl.when(p == 1)
                 def _():
-                    grads(s)
-                    router(s)
-
-            @pl.when(i == 4)
+                    hidden(s, 2)
+
+                for half in (0, 1):
+                    @pl.when(p == 2 + half)
+                    def _():
+                        grads(s, half, 2)
+                        router(s, half, 2)
+
+            @pl.when(i == 5)
             def _():
                 outer_sum()
 
-            @pl.when(i == 6)
+            @pl.when(i == 8)
             def _():
                 outer_own()
 
-            @pl.when(i == 8)
+            @pl.when(i == 10)
             def _():
                 outer_pass()
-        loop(10, step)
-
+
+            @pl.when(i == 15)
+            def _():
+                outer_half()
+        loop(18, step)
+
+        drains()
+        half_copy().wait_recv()
+        loop(16, lambda j: merge(j, lambda rows, half: scale * ACC[rows, HALF * half:HALF * (half + 1)]))
         qg_copy().wait_recv()
         Q[...] += QG[...]
 
@@ -411,54 +611,75 @@
 
     @pl.when(guest)
     def _():
-        ws = w_copies()
-
-        @pl.when((y == 0) | (y == 3))
-        def _():
-            for p in (0, 1):
-                line_drain(p, y)
-            ws[0].start()
-            outer_sum()
-            ws[0].wait_send()
-            ws[1].start()
-            outer_own()
-            ws[1].wait_send()
-            ws[2].start()
-            outer_pass()
-
-        @pl.when((y == 1) | (y == 2))
-        def _():
-            ws[0].start()
-            for i in (2, 3, 4, 5):
-                line_step(*item(i))
-            ws[0].wait_send()
-            ws[1].start()
-            outer_sum()
-            for i in (6, 7):
-                line_step(*item(i))
-            ws[1].wait_send()
-            ws[2].start()
-            outer_own()
-            outer_pass()
-        ws[0].wait_recv()
-        ws[1].wait_recv()
-        gg_copy().wait_recv()
-
-        def step(k):
-            s = item(2 * k)[1]
-            for col in (x, cx, px, ox):
-                arrived(0, s * 4 + col)
-            hidden(s)
-            for col in (x, cx, px, ox):
-                arrived(1, s * 4 + col)
-            grads(s)
-        loop(4, step)
-
-        GSND[...] = (scale * ACC[...]).astype(BF16)
-        gr_copy().start()
-        ws[2].wait_recv()
-        loop(4, router)
-        qg_copy().start()
+        outer_start()
+        for p in (0, 1):
+            line_drain(p, y)
+            line_send(p + 2, y)
+
+    @pl.when(guest & edge)
+    def _():
+        for p in (2, 3):
+            line_drain(p, y)
+        units = [w_unit(n, n, peer_e) for n in (0, 1)]
+        w_start(units[0][0])
+        w_start(units[1][0])
+        outer_sum()
+        w_sent(units[0][0])
+        w_sent(units[1][0])
+        units[0][1].start()
+        units[1][1].start()
+        outer_own()
+        outer_pass()
+        outer_half()
+        guest_work(1)
+
+    @pl.when(guest & mid)
+    def _():
+        to_edge = w_unit(0, 0, peer_e)
+        to_mid = w_unit(1, 2, other_e)
+        for i in range(4, 13):
+            if i == 6:
+                w_start(to_edge[0])
+                w_start(to_mid[0])
+            if i == 7:
+                outer_sum()
+            if i == 9:
+                outer_own()
+            if i == 11:
+                outer_pass()
+            line_step(*item(i))
+        w_sent(to_edge[0])
+        to_edge[1].start()
+        w_sent(to_mid[0])
+        to_mid[1].start()
+        guest_work(3)
+
+    @pl.when(guest)
+    def _():
+        drains()
+        half_copy().wait_recv()
+
+    @pl.when(guest & edge)
+    def _():
+        for half in (0, 1):
+            gr_to(half, 0, 0, 256, 0, e).wait_recv()
+
+    @pl.when(guest & mid)
+    def _():
+        for half in (0, 1):
+            gr_to(half, 0, 0, 128, 0, e).wait_recv()
+            gr_to(half, 1, 0, 128, 128, e).wait_recv()
+
+    @pl.when(guest)
+    def _():
+        loop(16, lambda j: merge(j, lambda rows, half: GRCV[half, rows].astype(F32)))
+
+    @pl.when(c != yh)
+    def _():
+        for copy in na_copies():
+            copy.wait_recv()
+        out_anc[...] = NAR[...]
+        out_mom[...] = NMR[...]
 
     def q_wait(j):
         @pl.when(home_of(j) != e)
@@ -470,67 +691,14 @@
     picked = PT[...] * (ebc * q1 + (1.0 - ebc) * q0)
     out_gate[...] = scale * jnp.sum(eye * jnp.sum(picked, axis=1, keepdims=True), axis=0, keepdims=True)
 
-    def ag_wait(j):
-        @pl.when(j != mj)
-        def _():
-            rc(AG.at[j], AG.at[j], ag_send.at[j], ag_recv.at[j], r, e).wait_recv()
-    loop(16, ag_wait)
-
-    @pl.when(c != yh)
-    def _():
-        for copy in na_copies():
-            copy.wait_recv()
-        out_anc[...] = NAR[...]
-        out_mom[...] = NMR[...]
-
-    own.wait()
-
-    def merge(j, grad):
-        rows = pl.ds(pl.multiple_of(16 * j, 16), 16)
-        out_frag[rows, :] = (MIX * Wo[rows, :].astype(F32) - MIX * INNER_RATE * grad(rows)
-                             + (1.0 - MIX) * AG[j].astype(F32)).astype(BF16)
-
-    @pl.when(home)
-    def _():
-        loop(16, lambda j: merge(j, lambda rows: scale * ACC[rows, :]))
-
-    @pl.when(guest)
-    def _():
-        gr_copy().wait_recv()
-        loop(16, lambda j: merge(j, lambda rows: GRCV[rows, :].astype(F32)))
-
-    def drain(i):
-        p, s = i // 4, i % 4
-
-        @pl.when(home | (y == 1) | (y == 2))
-        def _():
-            line_drain(p, s)
-
-        @pl.when(home)
-        def _():
-            to_partner(p, s).wait_send()
-            to_cross(p, s).wait_send()
-            on_to_partner(p, s).wait_send()
-            for col in range(4):
-                to_guest(p, s * 4 + col).wait_send()
-    loop(8, drain)
-
     def drain_small(j):
-        @pl.when(j != mj)
-        def _():
-            rs_copy(j).wait_send()
-            ag_copy(j).wait_send()
-
         @pl.when(home & (j != myslot))
         def _():
             q_copy(j).wait_send()
     loop(16, drain_small)
 
-    def drain_g(j):
-        @pl.when(home_of(j) != e)
-        def _():
-            g_copy(j).wait_send()
-    loop(8, drain_g)
+    ch_copy().wait_send()
+    half_copy().wait_send()
 
     @pl.when(home)
     def _():
@@ -538,9 +706,22 @@
 
     @pl.when(guest)
     def _():
-        w_copies()[2].wait_send()
-        gr_copy().wait_send()
         qg_copy().wait_send()
+
+    @pl.when(guest & edge)
+    def _():
+        for n in (0, 1):
+            w_unit(n, n, peer_e)[1].wait_send()
+        for half in (0, 1):
+            gr_edge(half).wait_send()
+
+    @pl.when(guest & mid)
+    def _():
+        w_unit(0, 0, peer_e)[1].wait_send()
+        w_unit(1, 2, other_e)[1].wait_send()
+        for half in (0, 1):
+            for copy in gr_mid(half):
+                copy.wait_send()
 
     @pl.when(owner)
     def _():
@@ -578,16 +759,16 @@
         in_specs=[vm] * 4 + [pl.BlockSpec(memory_space=pl.ANY)] * 3 + [vm] * 2,
         out_specs=[vm] * 4,
         scratch_shapes=[
-            V((2, 16, 128, D), BF16), V((2, 4, 128, D), BF16),
-            V((D, 256), BF16), V((D, 256), BF16), V((256, D), BF16), V((256, D), BF16),
-            V((4, 512, 256), BF16), V((256, D), F32), V((256, D), BF16), V((256, D), BF16), V((128, 128), F32),
-            V((16, 16, D), BF16), V((16, D), F32), V((16, D), BF16), V((16, D), BF16), V((16, 16, D), BF16),
+            V((4, 16, 128, D // 2), BF16), V((4, 4, 128, D // 2), BF16),
+            V((3, D, 256), BF16), V((3, 128, D), BF16), V((256, D), BF16),
+            V((4, 512, 384), BF16), V((384, D), F32), V((2, 384, D // 2), BF16), V((2, 256, D // 2), BF16), V((128, 128), F32),
+            V((128, D), BF16), V((8, 16, D), BF16), V((8, 16, D), BF16), V((16, D), F32), V((16, D), BF16), V((16, D), BF16), V((16, 16, D), BF16),
             V((8, D), F32), V((8, D), F32), V((8, D), F32), V((8, D), F32), V((8, D), F32), V((8, D), F32),
             V((2, 1, 128), F32), V((16, 1, 128), F32), V((16, 1, 128), F32), V((16, 1, 128), F32), V((8, 1, 128), F32),
-            dma((2, 4)), dma((2, 4)), dma((2, 4)), dma((2, 16)), dma((2, 4)), dma((2, 4)), dma((2, 4)), dma((2, 16)),
-            dma((3,)), dma((3,)),
+            dma((4, 4)), dma((4, 4)), dma((4, 4)), dma((4, 16)), dma((4, 4)), dma((4, 4)), dma((4, 4)), dma((4, 16)),
+            dma((3, 3)), dma((3, 3)),
             dma((8,)), dma((16,)), dma((16,)), dma((8,)), dma((16,)), dma((16,)), dma((16,)), dma((16,)),
-            dma((2,)), dma((2,)), dma((2,)), dma((2,)), dma((5,)), dma((5,)), dma((5,)),
+            dma((2,)), dma((2,)), dma((2,)), dma((2,)), dma((6,)), dma((6,)), dma((8,)), dma((2, 2)), dma((2, 2)),
         ],
         compiler_params=pltpu.CompilerParams(
             collective_id=0, has_side_effects=True, vmem_limit_bytes=58 * 1024 * 1024),

time: 106 us -> 102 us (0.962)
  Pallas kernels: 104 us -> 99.5 us
    pallas_call x1, Pallas kernels: 102 us -> 97.3 us  [per_device(): pl.pallas_call(kernel, out_shape=(jax.ShapeDtypeStruct((1, 128), F32), ja...]
where the time goes in v3:
time: 102 us; the launch traced here: 100 us
  Pallas kernels  99.5 us (98%)
    pallas_call x1, Pallas kernels, per_device(): pl.pallas_call(kernel, out_shape=(jax.ShapeDtypeStruct((1, 128), F32), ja...  97.3 us
    pallas_call x1, Pallas kernels, per_device(): pl.pallas_call(handover, out_shape=(jax.ShapeDtypeStruct((1, 128), F32),...  2.19 us

profile of v3, /device:TPU:1, one launch (start us, length us, event | category | flops | bytes accessed | tf_op | source)
XLA Modules:
  0.0 100.1 jit_solution(13937294128662869904)
XLA Ops:
  0.6 97.3 %step.1 = (f32[1,128]{1,0:T(1,128)}, bf16[256,1792]{1,0:T(8,128)(2,1)}, f32[8,1792]{1,0:T(8,128)}, f32[8,1792]{1,0:T(8,128)}) custom-call(bf16[128,1792]{1,0:T(8,128)(2,1)} %tok.1, bf16[128,1792]{1,0:T(8,128)(2,1)} %cot.1, s32[1,128]{1,0:T(1,128)} %bitcast.16, bf16[1,128]{1,0:T(2,128)(2,1)} %bitcast.17, bf16[1792,256]{1,0:T(8,128)(2,1)} %bitcast.11, ...), custom_call_target="tpu_custom_call" | custom-call | tf_op jit(solution)/shard_map/step/pallas_call | solution.py:751
  97.9 2.2 %handover.1 = (f32[1,128]{1,0:T(1,128)}, bf16[256,1792]{1,0:T(8,128)(2,1)}, f32[8,1792]{1,0:T(8,128)}, f32[8,1792]{1,0:T(8,128)}) custom-call(f32[1,128]{1,0:T(1,128)} %get-tuple-element.12.a, bf16[256,1792]{1,0:T(8,128)(2,1)} %get-tuple-element.13.b, f32[8,1792]{1,0:T(8,128)} %get-tuple-element.14.c, f32[8,1792]{1,0:T(8,128)} %get-tuple-element.15.d), custom_call_target="tpu_custom_call" | custom-call | tf_op jit(solution)/shard_map/handover/pallas_call | solution.py:777

commit v4 on v3

--- a/solution.py
+++ b/solution.py
@@ -20,9 +20,9 @@
 TN = (((0,), (0,)), ((), ()))
 
 
-def kernel(tok, cot, ids, gates, wg, wu, wd, anc, mom,
+def kernel(tok_in, cot_in, ids, gates, wg, wu, wd, anc, mom,
            out_gate, out_frag, out_anc, out_mom,
-           R, T, WU, WD, Wo, H, ACC, GSND, GRCV, PT,
+           tok, cot, R, T, WU, WD, Wo, H, ACC, GSND, GRCV, PT,
            CH, RSS, RS, TOT, PSS, PSR, AG, ANCR, MOMR, NAS, NMS, NAR, NMR,
            GSRC, GROW, Q, QG, QR,
            y_recv, y_up, y_dn, r_recv, xp_send, xc_send, xf_send, gu_send, w_send, w_recv,
@@ -82,6 +82,9 @@
 
     own = pltpu.make_async_copy(wd, Wo, l_sem.at[0])
     own.start()
+    rows_in = [pltpu.make_async_copy(a, b, l_sem.at[8 + n]) for n, (a, b) in enumerate(((tok_in, tok), (cot_in, cot)))]
+    for copy in rows_in:
+        copy.start()
 
     def w_local():
         pairs = []
@@ -133,9 +136,19 @@
     perm = (pos == lane.astype(F32)).astype(F32)
     PT[...] = perm
     permb = jnp.transpose(perm).astype(BF16)
+    for copy in rows_in:
+        copy.wait()
     for p, rows in enumerate((tok, tok, cot, cot)):
         cols = pl.ds(HALF * (p % 2), HALF)
-        T[p, y] = jnp.dot(permb, rows[:, cols], preferred_element_type=F32).astype(BF16)
+        part = jnp.dot(permb, rows[:, cols], preferred_element_type=F32).astype(BF16)
+
+        @pl.when(home)
+        def _(p=p, part=part):
+            R[p, myslot] = part
+
+        @pl.when(guest)
+        def _(p=p, part=part):
+            T[p, y] = part
     gp = perm * gcol
     g1 = jnp.sum(gp * ebc, axis=0, keepdims=True)
     g0 = jnp.sum(gp * (1.0 - ebc), axis=0, keepdims=True)
@@ -144,38 +157,48 @@
 
     pl.semaphore_wait(bar, 25 + y * (3 - y) // 2)
 
-    def up(p, s):
-        return rc(T.at[p, s], T.at[p, s], y_up.at[p, s], y_recv.at[p, s], r, e + 1)
-
-    def down(p, s):
-        return rc(T.at[p, s], T.at[p, s], y_dn.at[p, s], y_recv.at[p, s], r, e - 1)
-
-    def line_send(p, s):
+    def up(p, s, at_home):
+        a, b = R.at[p, s * 4 + x], T.at[p, s]
+        return rc(a if at_home else b, b if at_home else a, y_up.at[p, s], y_recv.at[p, s], r, e + 1)
+
+    def down(p, s, at_home):
+        a, b = R.at[p, s * 4 + x], T.at[p, s]
+        return rc(a if at_home else b, b if at_home else a, y_dn.at[p, s], y_recv.at[p, s], r, e - 1)
+
+    def line_send(p, s, at_home):
         @pl.when((s <= y) & (y < 2 + c))
         def _():
-            up(p, s).start()
+            up(p, s, at_home).start()
 
         @pl.when((s >= y) & (y > c))
         def _():
-            down(p, s).start()
-
-    def line_drain(p, s):
+            down(p, s, at_home).start()
+
+    def line_drain(p, s, at_home):
         @pl.when((s <= y) & (y < 2 + c))
         def _():
-            up(p, s).wait_send()
+            up(p, s, at_home).wait_send()
 
         @pl.when((s >= y) & (y > c))
         def _():
-            down(p, s).wait_send()
-
-    def line_step(p, s):
+            down(p, s, at_home).wait_send()
+
+    def line_step(p, s, at_home):
         @pl.when(((s < y) & (y <= 2 + c)) | ((s > y) & (y >= c)))
         def _():
-            rc(T.at[p, s], T.at[p, s], y_up.at[p, s], y_recv.at[p, s], r, e).wait_recv()
-        line_send(p, s)
-
-    line_send(0, y)
-    line_send(1, y)
+            got = R.at[p, s * 4 + x] if at_home else T.at[p, s]
+            rc(got, got, y_up.at[p, s], y_recv.at[p, s], r, e).wait_recv()
+        line_send(p, s, at_home)
+
+    @pl.when(guest)
+    def _():
+        line_send(0, y, False)
+        line_send(1, y, False)
+
+    @pl.when(home)
+    def _():
+        line_send(0, y, True)
+        line_send(1, y, True)
 
     def ch_copy():
         return rc(wd.at[pl.ds(pl.multiple_of(128 - 128 * c, 128), 128), :], CH, one_send.at[4], one_recv.at[4], mate, e)
@@ -303,26 +326,19 @@
 
     def to_partner(p, s):
         slot = s * 4 + x
-        return rc(T.at[p, s, win], R.at[p, slot, win], xp_send.at[p, s], r_recv.at[p, slot], r, px * 4 + y)
+        return rc(R.at[p, slot, win], R.at[p, slot, win], xp_send.at[p, s], r_recv.at[p, slot], r, px * 4 + y)
 
     def to_cross(p, s):
         slot = s * 4 + x
-        return rc(T.at[p, s, wot], R.at[p, slot, wot], xc_send.at[p, s], r_recv.at[p, slot], r, cx * 4 + y)
+        return rc(R.at[p, slot, wot], R.at[p, slot, wot], xc_send.at[p, s], r_recv.at[p, slot], r, cx * 4 + y)
 
     def on_to_partner(p, s):
         slot = s * 4 + cx
         return rc(R.at[p, slot, win], R.at[p, slot, win], xf_send.at[p, s], r_recv.at[p, slot], r, px * 4 + y)
 
-    def own_copy(p, s):
-        slot = s * 4 + x
-        return pltpu.make_async_copy(T.at[p, s, win], R.at[p, slot, win], r_recv.at[p, slot])
-
-    def to_guest(p, slot):
-        return rc(R.at[p, slot, win], R.at[p, slot, win], gu_send.at[p, slot], r_recv.at[p, slot], mate, e)
-
-    def own_to_guest(p, s):
-        slot = s * 4 + x
-        return rc(T.at[p, s, win], R.at[p, slot, win], gu_send.at[p, slot], r_recv.at[p, slot], mate, e)
+    def to_guest(p, s):
+        rows = R.at[p, pl.ds(s * 4, 4), win]
+        return rc(rows, rows, gu_send.at[p, s], r_recv.at[p, s * 4], mate, e)
 
     @pl.when(home)
     def _():
@@ -344,7 +360,15 @@
         GROW[myslot] = GSRC[x // 2]
 
     for p in range(4):
-        R[p, :, fill, :] = jnp.zeros((16, 32, HALF), BF16)
+        for k in range(4):
+            for d in (1, 2, 3):
+                R[p, 4 * k + (x + d) % 4, fill, :] = jnp.zeros((32, HALF), BF16)
+
+    @pl.when(guest)
+    def _():
+        for p in range(4):
+            for k in range(4):
+                R[p, 4 * k + x, fill, :] = jnp.zeros((32, HALF), BF16)
 
     def hidden(s, units):
         rows0 = R[0, pl.ds(s * 4, 4)].reshape(512, HALF)
@@ -416,24 +440,18 @@
         return rc(Q.at[slot], QR.at[x * 2 + y // 2], q_send.at[slot], q_recv.at[x * 2 + y // 2],
                   r, (slot % 4) * 4 + slot // 4)
 
-    def drain(i):
+    def drain(i, at_home):
         p, s = i // 4, i % 4
-
-        @pl.when(home | (mid & (s != y)))
-        def _():
-            line_drain(p, s)
-
-        @pl.when(guest & mid & (s == y) & (p > 1))
-        def _():
-            line_drain(p, s)
-
-        @pl.when(home)
-        def _():
+        if at_home:
+            line_drain(p, s, True)
             to_partner(p, s).wait_send()
             to_cross(p, s).wait_send()
             on_to_partner(p, s).wait_send()
-            for col in range(4):
-                to_guest(p, s * 4 + col).wait_send()
+            to_guest(p, s).wait_send()
+        else:
+            @pl.when(mid & ((s != y) | (p >= 2)))
+            def _():
+                line_drain(p, s, False)
 
     def drain_z(j):
         @pl.when(j != z)
@@ -445,8 +463,8 @@
         def _():
             g_copy(j).wait_send()
 
-    def drains():
-        loop(16, drain)
+    def drains(at_home):
+        loop(16, lambda i: drain(i, at_home))
         loop(8, drain_z)
         loop(8, drain_g)
 
@@ -466,15 +484,14 @@
                 for n in (13, 14, 15):
                     @pl.when(i == 4 * n - 48)
                     def _(n=n):
-                        line_step(*item(n))
+                        line_step(*item(n), False)
 
                 @pl.when(i == 10)
                 def _():
                     outer_half()
 
             p, s = item(i)
-            for col in (x, cx, px, ox):
-                arrived(p, s * 4 + col)
+            to_guest(p, s).wait_recv()
 
             @pl.when(p == 1)
             def _():
@@ -515,20 +532,12 @@
                 rc(GROW.at[slot], GROW.at[slot], g_send.at[0], g_recv.at[slot], r, e).wait_recv()
 
         def step(i):
-            @pl.when(i < 16)
-            def _():
-                p, s = item(i)
-                own_to_guest(p, s).start()
-                own_copy(p, s).start()
-
             @pl.when((i > 0) & (i < 17))
             def _():
                 p, s = item(i - 1)
                 arrived(p, s * 4 + cx)
                 on_to_partner(p, s).start()
-                to_guest(p, s * 4 + cx).start()
                 arrived(p, s * 4 + px)
-                to_guest(p, s * 4 + px).start()
 
             @pl.when(i == 1)
             def _():
@@ -536,15 +545,15 @@
 
             @pl.when(i == 2)
             def _():
-                line_send(2, y)
+                line_send(2, y, True)
 
             @pl.when(i == 4)
             def _():
-                line_send(3, y)
+                line_send(3, y, True)
 
             @pl.when((i > 2) & (i < 15))
             def _():
-                line_step(*item(i + 1))
+                line_step(*item(i + 1), True)
 
             @pl.when((i > 0) & (i < 15))
             def _():
@@ -566,8 +575,7 @@
             def _():
                 p, s = item(i - 2)
                 arrived(p, s * 4 + ox)
-                to_guest(p, s * 4 + ox).start()
-                own_copy(p, s).wait()
+                to_guest(p, s).start()
 
                 @pl.when(p == 1)
                 def _():
@@ -583,20 +591,20 @@
             def _():
                 outer_sum()
 
-            @pl.when(i == 8)
+            @pl.when(i == 7)
             def _():
                 outer_own()
 
-            @pl.when(i == 10)
+            @pl.when(i == 9)
             def _():
                 outer_pass()
 
-            @pl.when(i == 15)
+            @pl.when(i == 13)
             def _():
                 outer_half()
         loop(18, step)
 
-        drains()
+        drains(True)
         half_copy().wait_recv()
         loop(16, lambda j: merge(j, lambda rows, half: scale * ACC[rows, HALF * half:HALF * (half + 1)]))
         qg_copy().wait_recv()
@@ -613,23 +621,23 @@
     def _():
         outer_start()
         for p in (0, 1):
-            line_drain(p, y)
-            line_send(p + 2, y)
+            line_drain(p, y, False)
+            line_send(p + 2, y, False)
 
     @pl.when(guest & edge)
     def _():
         for p in (2, 3):
-            line_drain(p, y)
+            line_drain(p, y, False)
         units = [w_unit(n, n, peer_e) for n in (0, 1)]
-        w_start(units[0][0])
-        w_start(units[1][0])
-        outer_sum()
-        w_sent(units[0][0])
-        w_sent(units[1][0])
+        chain = [*units[0][0], *units[1][0]]
+        steps = (outer_sum, None, outer_own, outer_pass)
+        for copy, then in zip(chain, steps):
+            copy.start()
+            if then is not None:
+                then()
+            copy.wait_send()
         units[0][1].start()
         units[1][1].start()
-        outer_own()
-        outer_pass()
         outer_half()
         guest_work(1)
 
@@ -647,7 +655,7 @@
                 outer_own()
             if i == 11:
                 outer_pass()
-            line_step(*item(i))
+            line_step(*item(i), False)
         w_sent(to_edge[0])
         to_edge[1].start()
         w_sent(to_mid[0])
@@ -656,7 +664,7 @@
 
     @pl.when(guest)
     def _():
-        drains()
+        drains(False)
         half_copy().wait_recv()
 
     @pl.when(guest & edge)
@@ -756,10 +764,10 @@
             jax.ShapeDtypeStruct((8, D), F32),
             jax.ShapeDtypeStruct((8, D), F32),
         ),
-        in_specs=[vm] * 4 + [pl.BlockSpec(memory_space=pl.ANY)] * 3 + [vm] * 2,
+        in_specs=[pl.BlockSpec(memory_space=pl.ANY)] * 2 + [vm] * 2 + [pl.BlockSpec(memory_space=pl.ANY)] * 3 + [vm] * 2,
         out_specs=[vm] * 4,
         scratch_shapes=[
-            V((4, 16, 128, D // 2), BF16), V((4, 4, 128, D // 2), BF16),
+            V((128, D), BF16), V((128, D), BF16), V((4, 16, 128, D // 2), BF16), V((4, 4, 128, D // 2), BF16),
             V((3, D, 256), BF16), V((3, 128, D), BF16), V((256, D), BF16),
             V((4, 512, 384), BF16), V((384, D), F32), V((2, 384, D // 2), BF16), V((2, 256, D // 2), BF16), V((128, 128), F32),
             V((128, D), BF16), V((8, 16, D), BF16), V((8, 16, D), BF16), V((16, D), F32), V((16, D), BF16), V((16, D), BF16), V((16, 16, D), BF16),
@@ -768,7 +776,7 @@
             dma((4, 4)), dma((4, 4)), dma((4, 4)), dma((4, 16)), dma((4, 4)), dma((4, 4)), dma((4, 4)), dma((4, 16)),
             dma((3, 3)), dma((3, 3)),
             dma((8,)), dma((16,)), dma((16,)), dma((8,)), dma((16,)), dma((16,)), dma((16,)), dma((16,)),
-            dma((2,)), dma((2,)), dma((2,)), dma((2,)), dma((6,)), dma((6,)), dma((8,)), dma((2, 2)), dma((2, 2)),
+            dma((2,)), dma((2,)), dma((2,)), dma((2,)), dma((6,)), dma((6,)), dma((10,)), dma((2, 2)), dma((2, 2)),
         ],
         compiler_params=pltpu.CompilerParams(
             collective_id=0, has_side_effects=True, vmem_limit_bytes=58 * 1024 * 1024),

time: 102 us -> 101 us (level); the launches traced: 100 us -> 101 us
  no operation moved by 1% of the time
where the time goes in v4:
time: 101 us
  Pallas kernels  100 us (99%)
    pallas_call x1, Pallas kernels, per_device(): pl.pallas_call(kernel, out_shape=(jax.ShapeDtypeStruct((1, 128), F32), ja...  98 us
    pallas_call x1, Pallas kernels, per_device(): pl.pallas_call(handover, out_shape=(jax.ShapeDtypeStruct((1, 128), F32),...  2.19 us

profile of v4, /device:TPU:1, one launch (start us, length us, event | category | flops | bytes accessed | tf_op | source)
XLA Modules:
  0.0 100.8 jit_solution(14469512142484711559)
XLA Ops:
  0.6 98.0 %step.1 = (f32[1,128]{1,0:T(1,128)}, bf16[256,1792]{1,0:T(8,128)(2,1)}, f32[8,1792]{1,0:T(8,128)}, f32[8,1792]{1,0:T(8,128)}) custom-call(bf16[128,1792]{1,0:T(8,128)(2,1)} %tok_in.1, bf16[128,1792]{1,0:T(8,128)(2,1)} %cot_in.1, s32[1,128]{1,0:T(1,128)} %bitcast.16, bf16[1,128]{1,0:T(2,128)(2,1)} %bitcast.17, bf16[1792,256]{1,0:T(8,128)(2,1)} %bitcast.11, ...), custom_call_target="tpu_custom_call" | custom-call | tf_op jit(solution)/shard_map/step/pallas_call | solution.py:759
  98.6 2.2 %handover.1 = (f32[1,128]{1,0:T(1,128)}, bf16[256,1792]{1,0:T(8,128)(2,1)}, f32[8,1792]{1,0:T(8,128)}, f32[8,1792]{1,0:T(8,128)}) custom-call(f32[1,128]{1,0:T(1,128)} %get-tuple-element.12.a, bf16[256,1792]{1,0:T(8,128)(2,1)} %get-tuple-element.13.b, f32[8,1792]{1,0:T(8,128)} %get-tuple-element.14.c, f32[8,1792]{1,0:T(8,128)} %get-tuple-element.15.d), custom_call_target="tpu_custom_call" | custom-call | tf_op jit(solution)/shard_map/handover/pallas_call | solution.py:785
